TPU v7x, 1024 devices: a whole 4x8x16 slice. The times are simulated.
1024 devices in a mesh: fsdp: 256 (over y_lo, x, z), rep: 4 (over y_hi, core).
Axes of the slice: x: 4, y: 8 (y_hi: 2, y_lo: 4; y = y_hi * 4 + y_lo), z: 16, core: 2. Of those that a mesh axis runs over, the one named last changes fastest.
Arguments:
- tokens: bfloat16 [131072, 320], P(('fsdp', 'rep')), may hold values from -6 to 6
- weight: bfloat16 [16384, 6656], P('fsdp'), may hold values from -0.3125 to 0.3125
- cotangent: bfloat16 [131072, 6656], P(('fsdp', 'rep')), may hold values from -0.59765625 to 0.59765625
Outputs:
- token_grad: bfloat16 [131072, 320], P(('fsdp', 'rep'))
- weight_grad: bfloat16 [16384, 6656], P('fsdp')
All inputs are finite; a program needn't handle non-finite values.
Results may differ from a plain program's by a relative error of at most 0.013.
Values may be sent and summed in bfloat16 or wider, within the bound.
No kernel may reach another device: no remote copies, remote signals or barrier semaphores. Data moves between devices by JAX's collectives and lax.ppermute only.
A program may use at most 32 MiB of HBM per device.

v0:
```python
import jax
import jax.numpy as jnp
from jax import lax
from jax.sharding import PartitionSpec as P

HOPS = 2


def shifted(value, axis, steps):
    count = lax.axis_size(axis)
    pairs = [(source, (source + steps) % count) for source in range(count)]
    return lax.ppermute(value, axis, pairs)


def on_device(tokens, weight, cotangent):
    blocks_above = []
    blocks_below = []
    moving_up = weight
    moving_down = weight
    for offset in range(HOPS):
        moving_up = shifted(moving_up, "fsdp", -1)
        blocks_above.append(moving_up)
        moving_down = shifted(moving_down, "fsdp", 1)
        blocks_below.append(moving_down)
    ordered = blocks_below[::-1] + [weight] + blocks_above
    stacked = jnp.concatenate(ordered, axis=0)
    preact = jnp.dot(tokens, stacked, preferred_element_type=jnp.float32)
    logistic = jax.nn.sigmoid(preact)
    slope = (cotangent.astype(jnp.float32) * logistic * (1.0 + preact * (1.0 - logistic))).astype(
        jnp.bfloat16
    )
    token_grad = lax.dot_general(
        slope, stacked, (((1,), (1,)), ((), ())), preferred_element_type=jnp.float32
    ).astype(jnp.bfloat16)
    partials = lax.dot_general(
        tokens, slope, (((0,), (0,)), ((), ())), preferred_element_type=jnp.float32
    )
    partials = lax.optimization_barrier(partials.astype(jnp.bfloat16))
    shard_rows = weight.shape[0]
    partials = partials.reshape(2 * HOPS + 1, shard_rows, weight.shape[1])
    summed = partials[HOPS].astype(jnp.float32)
    for offset in range(1, HOPS + 1):
        from_lower = shifted(partials[HOPS + offset], "fsdp", offset)
        from_upper = shifted(partials[HOPS - offset], "fsdp", -offset)
        summed = summed + from_lower.astype(jnp.float32) + from_upper.astype(jnp.float32)
    group_grad = lax.optimization_barrier(summed.astype(jnp.bfloat16)).astype(jnp.float32)
    weight_grad = lax.psum(group_grad.astype(jnp.bfloat16), "rep")
    return (token_grad, weight_grad)


def solution(mesh):
    return jax.shard_map(
        on_device,
        mesh=mesh,
        in_specs=(P(("fsdp", "rep"), None), P("fsdp", None), P(("fsdp", "rep"), None)),
        out_specs=(P(("fsdp", "rep"), None), P("fsdp", None)),
        check_vma=False,
    )
```

profile of v0, /device:TPU:1, one launch (start us, length us, event | category | flops | bytes accessed | tf_op | source)
XLA Modules:
  0.0 235.6 jit_solution(16344967622867370919)
XLA Ops:
  7.2 0.0 copy-start
  7.2 0.0 copy-start.2
  7.2 0.0 all-reduce.2.cloned.1.call-start
  7.2 5.0 %collective-permute-start = (bf16[64,6656]{1,0:T(8,128)(2,1)}, bf16[64,6656]{1,0:T(8,128)(2,1)}, u32[]{:S(2)}, u32[]{:S(2)}) collective-permute-start(bf16[64,6656]{1,0:T(8,128)(2,1)} %param.4), channel_id=1, source_target_pairs={{0,4},{4,8},{8,12},{12,16},{16,20},{20,24},{24,28},{28,32},{32,36}... | collective-permute-start | bytes 2555912 | tf_op jit(solution)/shard_map/ppermute | solution.py:12
  12.2 21.1 %collective-permute-start.2 = (bf16[64,6656]{1,0:T(8,128)(2,1)}, bf16[64,6656]{1,0:T(8,128)(2,1)S(1)}, u32[]{:S(2)}, u32[]{:S(2)}) collective-permute-start(bf16[64,6656]{1,0:T(8,128)(2,1)} %param.4), channel_id=1, source_target_pairs={{0,1020},{4,0},{8,4},{12,8},{16,12},{20,16},{24,20},{28,24},{32,28... | collective-permute-start | bytes 2555912 | tf_op jit(solution)/shard_map/ppermute | solution.py:12
  33.3 17.0 %collective-permute-done = bf16[64,6656]{1,0:T(8,128)(2,1)} collective-permute-done((bf16[64,6656]{1,0:T(8,128)(2,1)}, bf16[64,6656]{1,0:T(8,128)(2,1)}, u32[]{:S(2)}, u32[]{:S(2)}) %collective-permute-start) | collective-permute-done | bytes 852000 | tf_op jit(solution)/shard_map/ppermute | solution.py:12
  50.4 1.9 collective-permute-start.1
  52.3 3.0 %copy.5 = bf16[128,6656]{0,1:T(8,128)(2,1)S(1)} copy(bf16[128,6656]{1,0:T(8,128)(2,1)} %param.5) | data formatting | bytes 3407872 | tf_op args[2]
  55.3 0.0 collective-permute-done.2
  55.3 9.4 %collective-permute-start.3 = (bf16[64,6656]{1,0:T(8,128)(2,1)S(1)}, bf16[64,6656]{1,0:T(8,128)(2,1)S(1)}, u32[]{:S(2)}, u32[]{:S(2)}) collective-permute-start(bf16[64,6656]{1,0:T(8,128)(2,1)S(1)} %collective-permute-done.2), channel_id=1, source_target_pairs={{0,1020},{4,0},{8,4},{12,8},{16,12},{20,16},{24,20},{28,24},{32,28... | collective-permute-start | bytes 2555912 | tf_op jit(solution)/shard_map/ppermute | solution.py:12
  64.7 13.1 %collective-permute-done.1 = bf16[64,6656]{1,0:T(8,128)(2,1)} collective-permute-done((bf16[64,6656]{1,0:T(8,128)(2,1)}, bf16[64,6656]{1,0:T(8,128)(2,1)}, u32[]{:S(2)}, u32[]{:S(2)}) %collective-permute-start.1) | collective-permute-done | bytes 852000 | tf_op jit(solution)/shard_map/ppermute | solution.py:12
  77.8 1.2 constant_dynamic-update-slice_fusion.4
  79.0 1.2 constant_dynamic-update-slice_fusion.3
  80.2 0.0 copy-done.2
  80.2 0.1 constant_dynamic-update-slice_fusion.2
  80.3 0.1 constant_dynamic-update-slice_fusion.1
  80.3 1.0 collective-permute-done.3
  81.4 0.1 constant_dynamic-update-slice_fusion
  81.5 0.0 copy-start.1
  81.5 2.0 copy-done.1
  83.4 0.0 copy-done
  83.4 2.1 multiply_convert_fusion
  85.6 1.3 fusion
  86.9 0.3 fusion.1
  87.1 4.1 %collective-permute-start.7 = (bf16[64,6656]{1,0:T(8,128)(2,1)S(1)}, bf16[64,6656]{1,0:T(8,128)(2,1)S(1)}, u32[]{:S(2)}, u32[]{:S(2)}) collective-permute-start(bf16[64,6656]{1,0:T(8,128)(2,1)S(1)} %get-tuple-element.3), channel_id=1, source_target_pairs={{0,1016},{4,1020},{8,0},{12,4},{16,8},{20,12},{24,16},{28,20},{32,... | collective-permute-start | bytes 2555912 | tf_op jit(solution)/shard_map/ppermute | solution.py:12
  91.3 2.1 collective-permute-start.6
  93.3 16.1 %collective-permute-start.5 = (bf16[64,6656]{1,0:T(8,128)(2,1)S(1)}, bf16[64,6656]{1,0:T(8,128)(2,1)S(1)}, u32[]{:S(2)}, u32[]{:S(2)}) collective-permute-start(bf16[64,6656]{1,0:T(8,128)(2,1)S(1)} %get-tuple-element.5), channel_id=1, source_target_pairs={{0,1020},{4,0},{8,4},{12,8},{16,12},{20,16},{24,20},{28,24},{32,28... | collective-permute-start | bytes 2555912 | tf_op jit(solution)/shard_map/ppermute | solution.py:12
  109.5 1.9 collective-permute-start.4
  111.4 15.4 %collective-permute-done.7 = bf16[64,6656]{1,0:T(8,128)(2,1)S(1)} collective-permute-done((bf16[64,6656]{1,0:T(8,128)(2,1)S(1)}, bf16[64,6656]{1,0:T(8,128)(2,1)S(1)}, u32[]{:S(2)}, u32[]{:S(2)}) %collective-permute-start.7) | collective-permute-done | bytes 852000 | tf_op jit(solution)/shard_map/ppermute | solution.py:12
  126.8 9.6 %collective-permute-done.6 = bf16[64,6656]{1,0:T(8,128)(2,1)S(1)} collective-permute-done((bf16[64,6656]{1,0:T(8,128)(2,1)S(1)}, bf16[64,6656]{1,0:T(8,128)(2,1)S(1)}, u32[]{:S(2)}, u32[]{:S(2)}) %collective-permute-start.6) | collective-permute-done | bytes 852000 | tf_op jit(solution)/shard_map/ppermute | solution.py:12
  136.4 14.1 %collective-permute-done.5 = bf16[64,6656]{1,0:T(8,128)(2,1)S(1)} collective-permute-done((bf16[64,6656]{1,0:T(8,128)(2,1)S(1)}, bf16[64,6656]{1,0:T(8,128)(2,1)S(1)}, u32[]{:S(2)}, u32[]{:S(2)}) %collective-permute-start.5) | collective-permute-done | bytes 852000 | tf_op jit(solution)/shard_map/ppermute | solution.py:12
  150.6 6.4 %collective-permute-done.4 = bf16[64,6656]{1,0:T(8,128)(2,1)S(1)} collective-permute-done((bf16[64,6656]{1,0:T(8,128)(2,1)S(1)}, bf16[64,6656]{1,0:T(8,128)(2,1)S(1)}, u32[]{:S(2)}, u32[]{:S(2)}) %collective-permute-start.4) | collective-permute-done | bytes 852000 | tf_op jit(solution)/shard_map/ppermute | solution.py:12
  157.0 1.4 add_convert_fusion
  158.4 0.0 all-reduce.2.cloned.1.call-update
  158.5 4.1 %convolution_convert_fusion.1 = bf16[128,320]{0,1:T(8,128)(2,1)} fusion(bf16[320,6656]{1,0:T(8,128)(2,1)} %copy-done.1, bf16[128,6656]{0,1:T(8,128)(2,1)S(1)} %multiply_convert_fusion), kind=kOutput, calls=%fused_computation.5 | convolution fusion | flops 545300480 | bytes 6045696 | tf_op jit(solution)/shard_map/dot_general | solution.py:32
  162.6 64.0 %all-reduce.2.cloned.1.call-done = bf16[64,6656]{1,0:T(8,128)(2,1)} async-done(((bf16[64,6656]{1,0:T(8,128)(2,1)}), bf16[64,6656]{1,0:T(8,128)(2,1)}) %all-reduce.2.cloned.1.call-update) | async-done | bytes 851984 | tf_op jit(solution)/shard_map/psum | solution.py:47
  226.6 2.1 copy.11
Async XLA Ops:
  7.2 76.3 %copy-start = (bf16[128,320]{0,1:T(8,128)(2,1)S(1)}, bf16[128,320]{0,1:T(8,128)(2,1)}, u32[]{:S(2)}) copy-start(bf16[128,320]{0,1:T(8,128)(2,1)} %param.3) | copy-start | bytes 245764
  7.2 73.0 %copy-start.2 = (bf16[64,6656]{1,0:T(8,128)(2,1)S(1)}, bf16[64,6656]{1,0:T(8,128)(2,1)}, u32[]{:S(2)}) copy-start(bf16[64,6656]{1,0:T(8,128)(2,1)} %param.4) | copy-start | bytes 2555908
  7.2 219.4 %all-reduce.2.cloned.1.call-start = ((), (), s32[]{:S(2)}) async-start(), calls=%async_computation | async-start | bytes 1703936 | tf_op jit(solution)/shard_map/psum | solution.py:47
  7.2 43.1 %collective-permute-start = (bf16[64,6656]{1,0:T(8,128)(2,1)}, bf16[64,6656]{1,0:T(8,128)(2,1)}, u32[]{:S(2)}, u32[]{:S(2)}) collective-permute-start(bf16[64,6656]{1,0:T(8,128)(2,1)} %param.4), channel_id=1, source_target_pairs={{0,4},{4,8},{8,12},{12,16},{16,20},{20,24},{24,28},{28,32},{32,36}... | collective-permute-start | bytes 2555912 | tf_op jit(solution)/shard_map/ppermute | solution.py:12
  12.2 43.1 %collective-permute-start.2 = (bf16[64,6656]{1,0:T(8,128)(2,1)}, bf16[64,6656]{1,0:T(8,128)(2,1)S(1)}, u32[]{:S(2)}, u32[]{:S(2)}) collective-permute-start(bf16[64,6656]{1,0:T(8,128)(2,1)} %param.4), channel_id=1, source_target_pairs={{0,1020},{4,0},{8,4},{12,8},{16,12},{20,16},{24,20},{28,24},{32,28... | collective-permute-start | bytes 2555912 | tf_op jit(solution)/shard_map/ppermute | solution.py:12
  50.4 27.4 %collective-permute-start.1 = (bf16[64,6656]{1,0:T(8,128)(2,1)}, bf16[64,6656]{1,0:T(8,128)(2,1)}, u32[]{:S(2)}, u32[]{:S(2)}) collective-permute-start(bf16[64,6656]{1,0:T(8,128)(2,1)} %collective-permute-done), channel_id=1, source_target_pairs={{0,4},{4,8},{8,12},{12,16},{16,20},{20,24},{24,28},{28,32},{32,36}... | collective-permute-start | bytes 2555912 | tf_op jit(solution)/shard_map/ppermute | solution.py:12
  55.3 26.1 %collective-permute-start.3 = (bf16[64,6656]{1,0:T(8,128)(2,1)S(1)}, bf16[64,6656]{1,0:T(8,128)(2,1)S(1)}, u32[]{:S(2)}, u32[]{:S(2)}) collective-permute-start(bf16[64,6656]{1,0:T(8,128)(2,1)S(1)} %collective-permute-done.2), channel_id=1, source_target_pairs={{0,1020},{4,0},{8,4},{12,8},{16,12},{20,16},{24,20},{28,24},{32,28... | collective-permute-start | bytes 2555912 | tf_op jit(solution)/shard_map/ppermute | solution.py:12
  81.5 2.0 copy-start.1
  87.1 39.7 %collective-permute-start.7 = (bf16[64,6656]{1,0:T(8,128)(2,1)S(1)}, bf16[64,6656]{1,0:T(8,128)(2,1)S(1)}, u32[]{:S(2)}, u32[]{:S(2)}) collective-permute-start(bf16[64,6656]{1,0:T(8,128)(2,1)S(1)} %get-tuple-element.3), channel_id=1, source_target_pairs={{0,1016},{4,1020},{8,0},{12,4},{16,8},{20,12},{24,16},{28,20},{32,... | collective-permute-start | bytes 2555912 | tf_op jit(solution)/shard_map/ppermute | solution.py:12
  91.3 45.2 %collective-permute-start.6 = (bf16[64,6656]{1,0:T(8,128)(2,1)S(1)}, bf16[64,6656]{1,0:T(8,128)(2,1)S(1)}, u32[]{:S(2)}, u32[]{:S(2)}) collective-permute-start(bf16[64,6656]{1,0:T(8,128)(2,1)S(1)} %get-tuple-element.4), channel_id=1, source_target_pairs={{0,8},{4,12},{8,16},{12,20},{16,24},{20,28},{24,32},{28,36},{32,40... | collective-permute-start | bytes 2555912 | tf_op jit(solution)/shard_map/ppermute | solution.py:12
  93.3 57.2 %collective-permute-start.5 = (bf16[64,6656]{1,0:T(8,128)(2,1)S(1)}, bf16[64,6656]{1,0:T(8,128)(2,1)S(1)}, u32[]{:S(2)}, u32[]{:S(2)}) collective-permute-start(bf16[64,6656]{1,0:T(8,128)(2,1)S(1)} %get-tuple-element.5), channel_id=1, source_target_pairs={{0,1020},{4,0},{8,4},{12,8},{16,12},{20,16},{24,20},{28,24},{32,28... | collective-permute-start | bytes 2555912 | tf_op jit(solution)/shard_map/ppermute | solution.py:12
  109.5 47.5 %collective-permute-start.4 = (bf16[64,6656]{1,0:T(8,128)(2,1)S(1)}, bf16[64,6656]{1,0:T(8,128)(2,1)S(1)}, u32[]{:S(2)}, u32[]{:S(2)}) collective-permute-start(bf16[64,6656]{1,0:T(8,128)(2,1)S(1)} %get-tuple-element.2), channel_id=1, source_target_pairs={{0,4},{4,8},{8,12},{12,16},{16,20},{20,24},{24,28},{28,32},{32,36}... | collective-permute-start | bytes 2555912 | tf_op jit(solution)/shard_map/ppermute | solution.py:12
Sparse Core Ops, SparseCore 0:
  158.6 67.9 all-reduce.1
where the time goes:
time: 236 us
  waiting for transfers between devices  141 us (60%)
  starting transfers between devices  61.6 us (26%)
  between operations  14.2 us (6%)
  local copies, waits for them, and re-layouts  9.98 us (4%)
  matrix products  7.51 us (3%)
    ppermute x8, waiting for transfers between devices, shifted(): return lax.ppermute(value, axis, pairs)  76.8 us
    psum x1, waiting for transfers between devices, on_device(): weight_grad = lax.psum(group_grad.astype(jnp.bfloat16), 'rep')  64 us
    ppermute x8, starting transfers between devices, shifted(): return lax.ppermute(value, axis, pairs)  61.6 us
    unnamed x12, local copies, waits for them, and re-layouts  9.65 us
  transfers between devices with their start and end apart: 9, of which 8 were waited for; matrix products, arithmetic and copies ran while one was open for 4% of the time, Pallas kernels for 0%

commit v1 on v0

v1 whole, which is shorter than its diff:
```python
import jax
import jax.numpy as jnp
from jax import lax
from jax.experimental import pallas as pl
from jax.experimental.pallas import tpu as pltpu
from jax.sharding import PartitionSpec as P

AXES = ("fsdp", "rep")
SPAN = 5


def _sub(width):
    cuts = list(range(0, width, 256)) + [width]
    return list(zip(cuts[:-1], cuts[1:]))


def gate_kernel(core, tok_t, w_a2, w_a1, w_0, w_b1, w_b2, cot_a, cot_b,
                p_a2, p_a1, p_0, p_b1, p_b2, tg, slope_s):
    del core
    tt = tok_t[...]
    tok = tt.T
    half = cot_a.shape[0]
    rows = w_0.shape[0]
    blocks = (w_a2, w_a1, w_0, w_b1, w_b2)
    outs = (p_a2, p_a1, p_0, p_b1, p_b2)
    for lo, hi in _sub(w_0.shape[1]):
        band = jnp.concatenate([w[:, lo:hi] for w in blocks], axis=0)
        pre = jnp.dot(tok, band, preferred_element_type=jnp.float32)
        s = 0.5 * jnp.tanh(0.5 * pre) + 0.5
        d = s * (1.0 + pre * (1.0 - s))
        up = jnp.concatenate([cot_a[:, lo:hi], cot_b[:, lo:hi]], axis=0)
        slope = (up.astype(jnp.float32) * d).astype(jnp.bfloat16)
        slope_s[:, lo:hi] = slope
        part = jnp.dot(tt, slope, preferred_element_type=jnp.float32)
        for k in range(SPAN):
            outs[k][:, lo:hi] = part[k * rows:(k + 1) * rows].astype(outs[k].dtype)
    band = jnp.concatenate([w[...] for w in blocks], axis=0)
    grad = lax.dot_general(band, slope_s[...], (((1,), (1,)), ((), ())),
                           preferred_element_type=jnp.float32)

    @pl.when(pl.program_id(0) == 0)
    def _():
        tg[...] = grad

    @pl.when(pl.program_id(0) > 0)
    def _():
        tg[...] += grad


def gate(core, tok_t, blocks, cotangent, cot_other, steps):
    shard, cols = blocks[0].shape
    width, both = tok_t.shape
    bc = cols // steps
    w_spec = pl.BlockSpec((shard, bc), lambda j, c: (0, j))
    c_own = pl.BlockSpec((both // 2, bc), lambda j, c: (0, c[0] * steps + j))
    c_oth = pl.BlockSpec((both // 2, bc), lambda j, c: (0, j))
    whole = pl.BlockSpec((width, both), lambda j, c: (0, 0))
    return pl.pallas_call(
        gate_kernel,
        grid_spec=pltpu.PrefetchScalarGridSpec(
            num_scalar_prefetch=1,
            grid=(steps,),
            in_specs=[whole] + [w_spec] * SPAN + [c_own, c_oth],
            out_specs=[w_spec] * SPAN + [whole],
            scratch_shapes=[pltpu.VMEM((both, bc), jnp.bfloat16)],
        ),
        out_shape=[jax.ShapeDtypeStruct((shard, cols), jnp.bfloat16)] * SPAN
        + [jax.ShapeDtypeStruct((width, both), jnp.float32)],
        compiler_params=pltpu.CompilerParams(vmem_limit_bytes=32 * 1024 * 1024),
        cost_estimate=pl.CostEstimate(
            flops=6 * width * both * cols, bytes_accessed=6 * 1024 * 1024, transcendentals=both * cols
        ),
    )(core, tok_t, *blocks, cotangent, cot_other)


def solution(mesh):
    n_f, n_r = mesh.shape["fsdp"], mesh.shape["rep"]

    def pairs(move):
        out = []
        for p in range(n_f):
            for r in range(n_r):
                q, t = move(p, r)
                out.append((p * n_r + r, (q % n_f) * n_r + t))
        return out

    ring_a = pairs(lambda p, r: (p + (1 if r % 2 == 0 else -1), r))
    ring_b = pairs(lambda p, r: (p + (-1 if r % 2 == 0 else 1), r))
    swap_core = pairs(lambda p, r: (p, r ^ 1))
    swap_far = pairs(lambda p, r: (p, r ^ 2))
    core_groups = [[g, g + 1] for g in range(0, n_r, 2)]

    def on_device(tokens, weight, cotangent):
        core = lax.axis_index("rep") % 2
        shard, f = weight.shape
        cols = f // 2
        rows = tokens.shape[0]

        def flip(t):
            back = t.reshape(SPAN, shard, t.shape[1])[::-1].reshape(t.shape)
            return jnp.where(core == 0, t, back)

        send = lambda v, how: lax.ppermute(v, AXES, how)
        w_0 = lax.dynamic_slice(weight, (0, core * cols), (shard, cols))
        w_a1 = send(w_0, ring_a)
        w_b1 = send(w_0, ring_b)
        w_a2 = send(w_a1, ring_a)
        w_b2 = send(w_b1, ring_b)
        cot_out = lax.dynamic_slice(cotangent, (0, (1 - core) * cols), (rows, cols))
        cot_other = send(cot_out, swap_core)
        tok_own = tokens.T
        tok_other = send(tok_own, swap_core)
        tok_t = flip(jnp.concatenate([tok_own, tok_other], axis=1))
        p_a2, p_a1, p_0, p_b1, p_b2, tg = gate(
            core.reshape(1).astype(jnp.int32), tok_t, (w_a2, w_a1, w_0, w_b1, w_b2),
            cotangent, cot_other, 2)
        f32 = lambda v: v.astype(jnp.float32)
        g_a = send(p_b2, ring_a)
        g_b = send(p_a2, ring_b)
        g_a = send((f32(g_a) + f32(p_b1)).astype(jnp.bfloat16), ring_a)
        g_b = send((f32(g_b) + f32(p_a1)).astype(jnp.bfloat16), ring_b)
        mine = (f32(p_0) + f32(g_a) + f32(g_b)).astype(jnp.bfloat16)
        far = send(mine, swap_far)
        half = (f32(mine) + f32(far)).astype(jnp.bfloat16)
        weight_grad = lax.all_gather(half, "rep", axis=1, tiled=True, axis_index_groups=core_groups)
        tg = flip(tg)
        tg_other = send(tg[:, rows:], swap_core)
        token_grad = (tg[:, :rows] + tg_other).astype(jnp.bfloat16).T
        return (token_grad, weight_grad)

    return jax.shard_map(
        on_device,
        mesh=mesh,
        in_specs=(P(AXES, None), P("fsdp", None), P(AXES, None)),
        out_specs=(P(AXES, None), P("fsdp", None)),
        check_vma=False,
    )
```

time: 236 us -> 134 us (0.57)
  waiting for transfers between devices: 141 us -> 44.7 us
  between operations: 14.2 us -> 0.9 us
  starting transfers between devices: 61.6 us -> 71.7 us
  matrix products: 7.51 us -> 0 us
  Pallas kernels: 0 us -> 6.68 us
  local copies, waits for them, and re-layouts: 9.98 us -> 4.24 us
  blocking collectives: 0 us -> 2.42 us
    psum x1 -> x0, waiting for transfers between devices: 64 us -> none  [on_device(): weight_grad = lax.psum(group_grad.astype(jnp.bfloat16), 'rep')]
    ppermute x8 -> x12, waiting for transfers between devices: 76.8 us -> 44.7 us  [on_device(): send = lambda v, how: lax.ppermute(v, AXES, how)]
    ppermute x8 -> x12, starting transfers between devices: 61.6 us -> 71.7 us  [on_device(): send = lambda v, how: lax.ppermute(v, AXES, how)]
    unnamed x12 -> x9, local copies, waits for them, and re-layouts: 9.65 us -> 2.04 us
    dot_general x3 -> x0, matrix products: 7.51 us -> none  [the longest x1 4.11 us: on_device(): lax.dot_general(slope, stacked, (((1,), (1,)), ((), ())), preferred_eleme...]
    pallas_call x0 -> x1, Pallas kernels: none -> 6.68 us  [gate(): pl.pallas_call(gate_kernel, grid_spec=pltpu.PrefetchScalarGridSpec(num_sc...]
    all_gather x0 -> x1, blocking collectives: none -> 2.42 us  [on_device(): lax.all_gather(half, 'rep', axis=1, tiled=True, axis_index_groups=core_gr...]
  transfers between devices with their start and end apart: 9 -> 12, of which waited for: 8 -> 8; matrix products, arithmetic and copies ran while one was open for 4% -> 2% of each run, Pallas kernels for 0% -> 0%
where the time goes in v1:
time: 134 us; the launch traced here: 133 us
  starting transfers between devices  71.7 us (54%)
  waiting for transfers between devices  44.7 us (33%)
  Pallas kernels  6.68 us (5%)
  local copies, waits for them, and re-layouts  4.24 us (3%)
  blocking collectives  2.42 us (2%)
  other arithmetic  2.23 us (2%)
    ppermute x12, starting transfers between devices, on_device(): send = lambda v, how: lax.ppermute(v, AXES, how)  71.7 us
    ppermute x12, waiting for transfers between devices, on_device(): send = lambda v, how: lax.ppermute(v, AXES, how)  44.7 us
    pallas_call x1, Pallas kernels, gate(): pl.pallas_call(gate_kernel, grid_spec=pltpu.PrefetchScalarGridSpec(num_sc...  6.68 us
  transfers between devices with their start and end apart: 12, of which 8 were waited for; matrix products, arithmetic and copies ran while one was open for 2% of the time, Pallas kernels for 0%

profile of v1, /device:TPU:1, one launch (start us, length us, event | category | flops | bytes accessed | tf_op | source)
XLA Modules:
  0.0 132.9 jit_solution(10576766532654125273)
XLA Ops:
  0.6 0.0 copy-start
  0.6 0.0 copy-start.3
  0.7 1.1 copy-done
  1.8 0.0 copy-start.1
  1.8 5.0 %collective-permute-start.3 = (bf16[64,3328]{1,0:T(8,128)(2,1)S(1)}, bf16[64,3328]{1,0:T(8,128)(2,1)}, u32[]{:S(2)}, u32[]{:S(2)}) collective-permute-start(bf16[64,3328]{1,0:T(8,128)(2,1)S(1)} %constant_dynamic-slice_fusion.1.w_0), channel_id=1, source_target_pairs={{0,1020},{1,5},{2,1022},{3,7},{4,0},{5,9},{6,2},{7,11},{8,4},{9,13... | collective-permute-start | bytes 1277960 | tf_op jit(solution)/shard_map/ppermute | solution.py:103
  6.8 21.1 %collective-permute-start.1 = (bf16[64,3328]{1,0:T(8,128)(2,1)S(1)}, bf16[64,3328]{1,0:T(8,128)(2,1)}, u32[]{:S(2)}, u32[]{:S(2)}) collective-permute-start(bf16[64,3328]{1,0:T(8,128)(2,1)S(1)} %constant_dynamic-slice_fusion.1.w_0), channel_id=1, source_target_pairs={{0,4},{1,1021},{2,6},{3,1023},{4,8},{5,1},{6,10},{7,3},{8,12},{9,5... | collective-permute-start | bytes 1277960 | tf_op jit(solution)/shard_map/ppermute | solution.py:103
  27.9 2.1 %constant_dynamic-slice_fusion = bf16[128,3328]{1,0:T(8,128)(2,1)} fusion(bf16[128,6656]{1,0:T(8,128)(2,1)} %cot_a.1, s32[]{:T(128)S(6)} %select_n.31), kind=kLoop, calls=%fused_computation.10 | loop fusion | bytes 1703940 | tf_op jit(solution)/shard_map/dynamic_slice | solution.py:109
  30.0 2.9 %collective-permute-start.5 = (bf16[128,3328]{1,0:T(8,128)(2,1)}, bf16[128,3328]{1,0:T(8,128)(2,1)}, u32[]{:S(2)}, u32[]{:S(2)}) collective-permute-start(bf16[128,3328]{1,0:T(8,128)(2,1)} %constant_dynamic-slice_fusion), channel_id=1, source_target_pairs={{0,1},{1,0},{2,3},{3,2},{4,5},{5,4},{6,7},{7,6},{8,9},{9,8},{10,11... | collective-permute-start | bytes 2555912 | tf_op jit(solution)/shard_map/ppermute | solution.py:103
  32.9 0.0 copy-done.3
  32.9 1.9 %collective-permute-start = (bf16[320,128]{1,0:T(8,128)(2,1)S(1)}, bf16[320,128]{1,0:T(8,128)(2,1)S(1)}, u32[]{:S(2)}, u32[]{:S(2)}) collective-permute-start(bf16[320,128]{1,0:T(8,128)(2,1)S(1)} %bitcast.12), channel_id=1, source_target_pairs={{0,1},{1,0},{2,3},{3,2},{4,5},{5,4},{6,7},{7,6},{8,9},{9,8},{10,11... | collective-permute-start | bytes 245768 | tf_op jit(solution)/shard_map/ppermute | solution.py:103
  34.8 0.0 collective-permute-done.3.w_b1
  34.8 1.9 %collective-permute-start.4 = (bf16[64,3328]{1,0:T(8,128)(2,1)}, bf16[64,3328]{1,0:T(8,128)(2,1)}, u32[]{:S(2)}, u32[]{:S(2)}) collective-permute-start(bf16[64,3328]{1,0:T(8,128)(2,1)} %collective-permute-done.3.w_b1), channel_id=1, source_target_pairs={{0,1020},{1,5},{2,1022},{3,7},{4,0},{5,9},{6,2},{7,11},{8,4},{9,13... | collective-permute-start | bytes 1277960 | tf_op jit(solution)/shard_map/ppermute | solution.py:103
  36.8 0.0 collective-permute-done.1.w_a1
  36.8 9.9 %collective-permute-start.2 = (bf16[64,3328]{1,0:T(8,128)(2,1)}, bf16[64,3328]{1,0:T(8,128)(2,1)}, u32[]{:S(2)}, u32[]{:S(2)}) collective-permute-start(bf16[64,3328]{1,0:T(8,128)(2,1)} %collective-permute-done.1.w_a1), channel_id=1, source_target_pairs={{0,4},{1,1021},{2,6},{3,1023},{4,8},{5,1},{6,10},{7,3},{8,12},{9,5... | collective-permute-start | bytes 1277960 | tf_op jit(solution)/shard_map/ppermute | solution.py:103
  46.7 0.0 collective-permute-done
  46.7 0.1 bitcast_select_fusion.1.tok_t
  46.8 3.5 %collective-permute-done.4.w_b2 = bf16[64,3328]{1,0:T(8,128)(2,1)} collective-permute-done((bf16[64,3328]{1,0:T(8,128)(2,1)}, bf16[64,3328]{1,0:T(8,128)(2,1)}, u32[]{:S(2)}, u32[]{:S(2)}) %collective-permute-start.4) | collective-permute-done | bytes 426016 | tf_op jit(solution)/shard_map/ppermute | solution.py:103
  50.3 6.0 %collective-permute-done.2.w_a2 = bf16[64,3328]{1,0:T(8,128)(2,1)} collective-permute-done((bf16[64,3328]{1,0:T(8,128)(2,1)}, bf16[64,3328]{1,0:T(8,128)(2,1)}, u32[]{:S(2)}, u32[]{:S(2)}) %collective-permute-start.2) | collective-permute-done | bytes 426016 | tf_op jit(solution)/shard_map/ppermute | solution.py:103
  56.3 0.0 collective-permute-done.5.cot_b
  56.3 0.0 copy-done.1
  56.3 6.7 %shard_map.50 = (bf16[64,3328]{1,0:T(8,128)(2,1)S(1)}, bf16[64,3328]{1,0:T(8,128)(2,1)S(1)}, bf16[64,3328]{1,0:T(8,128)(2,1)S(1)}, bf16[64,3328]{1,0:T(8,128)(2,...) custom-call(s32[1]{0:T(128)} %bitcast.core, bf16[320,256]{1,0:T(8,128)(2,1)S(1)} %bitcast_select_fusion.1.tok_t, ...), custom_call_target="tpu_custom_call" | custom-call | flops 1635778560 | bytes 6291456 | tf_op jit(solution)/shard_map/pallas_call | solution.py:58
  63.0 0.0 copy-start.2
  63.0 10.1 %collective-permute-start.7 = (bf16[64,3328]{1,0:T(8,128)(2,1)S(1)}, bf16[64,3328]{1,0:T(8,128)(2,1)S(1)}, u32[]{:S(2)}, u32[]{:S(2)}) collective-permute-start(bf16[64,3328]{1,0:T(8,128)(2,1)S(1)} %get-tuple-element.10), channel_id=1, source_target_pairs={{0,4},{1,1021},{2,6},{3,1023},{4,8},{5,1},{6,10},{7,3},{8,12},{9,5... | collective-permute-start | bytes 1277960 | tf_op jit(solution)/shard_map/ppermute | solution.py:103
  73.1 1.9 %collective-permute-start.9 = (bf16[64,3328]{1,0:T(8,128)(2,1)S(1)}, bf16[64,3328]{1,0:T(8,128)(2,1)S(1)}, u32[]{:S(2)}, u32[]{:S(2)}) collective-permute-start(bf16[64,3328]{1,0:T(8,128)(2,1)S(1)} %get-tuple-element.12), channel_id=1, source_target_pairs={{0,1020},{1,5},{2,1022},{3,7},{4,0},{5,9},{6,2},{7,11},{8,4},{9,13... | collective-permute-start | bytes 1277960 | tf_op jit(solution)/shard_map/ppermute | solution.py:103
  75.1 3.1 %collective-permute-done.7 = bf16[64,3328]{1,0:T(8,128)(2,1)S(1)} collective-permute-done((bf16[64,3328]{1,0:T(8,128)(2,1)S(1)}, bf16[64,3328]{1,0:T(8,128)(2,1)S(1)}, u32[]{:S(2)}, u32[]{:S(2)}) %collective-permute-start.7) | collective-permute-done | bytes 426016 | tf_op jit(solution)/shard_map/ppermute | solution.py:103
  78.2 0.1 add_convert_fusion.3
  78.3 9.8 %collective-permute-start.8 = (bf16[64,3328]{1,0:T(8,128)(2,1)S(1)}, bf16[64,3328]{1,0:T(8,128)(2,1)S(1)}, u32[]{:S(2)}, u32[]{:S(2)}) collective-permute-start(bf16[64,3328]{1,0:T(8,128)(2,1)S(1)} %add_convert_fusion.3), channel_id=1, source_target_pairs={{0,4},{1,1021},{2,6},{3,1023},{4,8},{5,1},{6,10},{7,3},{8,12},{9,5... | collective-permute-start | bytes 1277960 | tf_op jit(solution)/shard_map/ppermute | solution.py:103
  88.1 1.7 %collective-permute-done.9 = bf16[64,3328]{1,0:T(8,128)(2,1)S(1)} collective-permute-done((bf16[64,3328]{1,0:T(8,128)(2,1)S(1)}, bf16[64,3328]{1,0:T(8,128)(2,1)S(1)}, u32[]{:S(2)}, u32[]{:S(2)}) %collective-permute-start.9) | collective-permute-done | bytes 426016 | tf_op jit(solution)/shard_map/ppermute | solution.py:103
  89.9 0.1 add_convert_fusion.2
  90.0 0.0 copy-done.2
  90.0 1.9 %collective-permute-start.10 = (bf16[64,3328]{1,0:T(8,128)(2,1)S(1)}, bf16[64,3328]{1,0:T(8,128)(2,1)S(1)}, u32[]{:S(2)}, u32[]{:S(2)}) collective-permute-start(bf16[64,3328]{1,0:T(8,128)(2,1)S(1)} %add_convert_fusion.2), channel_id=1, source_target_pairs={{0,1020},{1,5},{2,1022},{3,7},{4,0},{5,9},{6,2},{7,11},{8,4},{9,13... | collective-permute-start | bytes 1277960 | tf_op jit(solution)/shard_map/ppermute | solution.py:103
  91.9 1.2 collective-permute-done.8
  93.2 19.0 %collective-permute-done.10 = bf16[64,3328]{1,0:T(8,128)(2,1)S(1)} collective-permute-done((bf16[64,3328]{1,0:T(8,128)(2,1)S(1)}, bf16[64,3328]{1,0:T(8,128)(2,1)S(1)}, u32[]{:S(2)}, u32[]{:S(2)}) %collective-permute-start.10) | collective-permute-done | bytes 426016 | tf_op jit(solution)/shard_map/ppermute | solution.py:103
  112.2 1.2 add_convert_fusion.1
  113.4 3.4 %collective-permute-start.11 = (bf16[64,3328]{1,0:T(8,128)(2,1)S(1)}, bf16[64,3328]{1,0:T(8,128)(2,1)S(1)}, u32[]{:S(2)}, u32[]{:S(2)}) collective-permute-start(bf16[64,3328]{1,0:T(8,128)(2,1)S(1)} %add_convert_fusion.1), channel_id=1, source_target_pairs={{0,2},{1,3},{2,0},{3,1},{4,6},{5,7},{6,4},{7,5},{8,10},{9,11},{10,... | collective-permute-start | bytes 1277960 | tf_op jit(solution)/shard_map/ppermute | solution.py:103
  116.8 1.9 %collective-permute-start.6 = (f32[320,128]{1,0:T(8,128)S(1)}, f32[320,128]{1,0:T(8,128)S(1)}, u32[]{:S(2)}, u32[]{:S(2)}) collective-permute-start(f32[320,128]{1,0:T(8,128)S(1)} %slice.9), channel_id=1, source_target_pairs={{0,1},{1,0},{2,3},{3,2},{4,5},{5,4},{6,7},{7,6},{8,9},{9,8},{10,11... | collective-permute-start | bytes 491528 | tf_op jit(solution)/shard_map/ppermute | solution.py:103
  118.8 1.4 %collective-permute-done.6 = f32[320,128]{1,0:T(8,128)S(1)} collective-permute-done((f32[320,128]{1,0:T(8,128)S(1)}, f32[320,128]{1,0:T(8,128)S(1)}, u32[]{:S(2)}, u32[]{:S(2)}) %collective-permute-start.6) | collective-permute-done | bytes 163872 | tf_op jit(solution)/shard_map/ppermute | solution.py:103
  120.1 0.7 fusion.1
  120.8 8.7 %collective-permute-done.11 = bf16[64,3328]{1,0:T(8,128)(2,1)S(1)} collective-permute-done((bf16[64,3328]{1,0:T(8,128)(2,1)S(1)}, bf16[64,3328]{1,0:T(8,128)(2,1)S(1)}, u32[]{:S(2)}, u32[]{:S(2)}) %collective-permute-start.11) | collective-permute-done | bytes 426016 | tf_op jit(solution)/shard_map/ppermute | solution.py:103
  129.5 0.1 add_convert_fusion
  129.6 2.4 %all_gather.3 = bf16[64,6656]{1,0:T(8,128)(2,1)S(1)} all-gather(bf16[64,3328]{1,0:T(8,128)(2,1)S(1)} %add_convert_fusion), channel_id=1, replica_groups={{0,1},{2,3},{4,5},{6,7},{8,9},{10,11},{12,13},{14,15},{16,17},{18,19},{..., dimensions={1}, use_global_device_ids=true | all-gather | bytes 1277952 | tf_op jit(solution)/shard_map/all_gather | solution.py:125
  132.0 0.9 copy.6
  (6 shorter events, 0.1 us)
Async XLA Ops:
  0.6 1.2 copy-start
  0.6 32.2 %copy-start.3 = (bf16[128,320]{0,1:T(8,128)(2,1)S(1)}, bf16[128,320]{0,1:T(8,128)(2,1)}, u32[]{:S(2)}) copy-start(bf16[128,320]{0,1:T(8,128)(2,1)} %param.3) | copy-start | bytes 245764
  1.8 54.5 %copy-start.1 = (bf16[128,6656]{1,0:T(8,128)(2,1)S(1)}, bf16[128,6656]{1,0:T(8,128)(2,1)}, u32[]{:S(2)}) copy-start(bf16[128,6656]{1,0:T(8,128)(2,1)} %cot_a.1) | copy-start | bytes 5111812
  1.8 33.0 %collective-permute-start.3 = (bf16[64,3328]{1,0:T(8,128)(2,1)S(1)}, bf16[64,3328]{1,0:T(8,128)(2,1)}, u32[]{:S(2)}, u32[]{:S(2)}) collective-permute-start(bf16[64,3328]{1,0:T(8,128)(2,1)S(1)} %constant_dynamic-slice_fusion.1.w_0), channel_id=1, source_target_pairs={{0,1020},{1,5},{2,1022},{3,7},{4,0},{5,9},{6,2},{7,11},{8,4},{9,13... | collective-permute-start | bytes 1277960 | tf_op jit(solution)/shard_map/ppermute | solution.py:103
  6.8 30.0 %collective-permute-start.1 = (bf16[64,3328]{1,0:T(8,128)(2,1)S(1)}, bf16[64,3328]{1,0:T(8,128)(2,1)}, u32[]{:S(2)}, u32[]{:S(2)}) collective-permute-start(bf16[64,3328]{1,0:T(8,128)(2,1)S(1)} %constant_dynamic-slice_fusion.1.w_0), channel_id=1, source_target_pairs={{0,4},{1,1021},{2,6},{3,1023},{4,8},{5,1},{6,10},{7,3},{8,12},{9,5... | collective-permute-start | bytes 1277960 | tf_op jit(solution)/shard_map/ppermute | solution.py:103
  30.0 26.3 %collective-permute-start.5 = (bf16[128,3328]{1,0:T(8,128)(2,1)}, bf16[128,3328]{1,0:T(8,128)(2,1)}, u32[]{:S(2)}, u32[]{:S(2)}) collective-permute-start(bf16[128,3328]{1,0:T(8,128)(2,1)} %constant_dynamic-slice_fusion), channel_id=1, source_target_pairs={{0,1},{1,0},{2,3},{3,2},{4,5},{5,4},{6,7},{7,6},{8,9},{9,8},{10,11... | collective-permute-start | bytes 2555912 | tf_op jit(solution)/shard_map/ppermute | solution.py:103
  32.9 13.8 %collective-permute-start = (bf16[320,128]{1,0:T(8,128)(2,1)S(1)}, bf16[320,128]{1,0:T(8,128)(2,1)S(1)}, u32[]{:S(2)}, u32[]{:S(2)}) collective-permute-start(bf16[320,128]{1,0:T(8,128)(2,1)S(1)} %bitcast.12), channel_id=1, source_target_pairs={{0,1},{1,0},{2,3},{3,2},{4,5},{5,4},{6,7},{7,6},{8,9},{9,8},{10,11... | collective-permute-start | bytes 245768 | tf_op jit(solution)/shard_map/ppermute | solution.py:103
  34.8 15.5 %collective-permute-start.4 = (bf16[64,3328]{1,0:T(8,128)(2,1)}, bf16[64,3328]{1,0:T(8,128)(2,1)}, u32[]{:S(2)}, u32[]{:S(2)}) collective-permute-start(bf16[64,3328]{1,0:T(8,128)(2,1)} %collective-permute-done.3.w_b1), channel_id=1, source_target_pairs={{0,1020},{1,5},{2,1022},{3,7},{4,0},{5,9},{6,2},{7,11},{8,4},{9,13... | collective-permute-start | bytes 1277960 | tf_op jit(solution)/shard_map/ppermute | solution.py:103
  36.8 19.5 %collective-permute-start.2 = (bf16[64,3328]{1,0:T(8,128)(2,1)}, bf16[64,3328]{1,0:T(8,128)(2,1)}, u32[]{:S(2)}, u32[]{:S(2)}) collective-permute-start(bf16[64,3328]{1,0:T(8,128)(2,1)} %collective-permute-done.1.w_a1), channel_id=1, source_target_pairs={{0,4},{1,1021},{2,6},{3,1023},{4,8},{5,1},{6,10},{7,3},{8,12},{9,5... | collective-permute-start | bytes 1277960 | tf_op jit(solution)/shard_map/ppermute | solution.py:103
  63.0 27.0 %copy-start.2 = (bf16[64,3328]{1,0:T(8,128)(2,1)}, bf16[64,3328]{1,0:T(8,128)(2,1)S(1)}, u32[]{:S(2)}) copy-start(bf16[64,3328]{1,0:T(8,128)(2,1)S(1)} %get-tuple-element.9) | copy-start | bytes 1277956
  63.0 15.2 %collective-permute-start.7 = (bf16[64,3328]{1,0:T(8,128)(2,1)S(1)}, bf16[64,3328]{1,0:T(8,128)(2,1)S(1)}, u32[]{:S(2)}, u32[]{:S(2)}) collective-permute-start(bf16[64,3328]{1,0:T(8,128)(2,1)S(1)} %get-tuple-element.10), channel_id=1, source_target_pairs={{0,4},{1,1021},{2,6},{3,1023},{4,8},{5,1},{6,10},{7,3},{8,12},{9,5... | collective-permute-start | bytes 1277960 | tf_op jit(solution)/shard_map/ppermute | solution.py:103
  73.1 16.7 %collective-permute-start.9 = (bf16[64,3328]{1,0:T(8,128)(2,1)S(1)}, bf16[64,3328]{1,0:T(8,128)(2,1)S(1)}, u32[]{:S(2)}, u32[]{:S(2)}) collective-permute-start(bf16[64,3328]{1,0:T(8,128)(2,1)S(1)} %get-tuple-element.12), channel_id=1, source_target_pairs={{0,1020},{1,5},{2,1022},{3,7},{4,0},{5,9},{6,2},{7,11},{8,4},{9,13... | collective-permute-start | bytes 1277960 | tf_op jit(solution)/shard_map/ppermute | solution.py:103
  78.3 14.9 %collective-permute-start.8 = (bf16[64,3328]{1,0:T(8,128)(2,1)S(1)}, bf16[64,3328]{1,0:T(8,128)(2,1)S(1)}, u32[]{:S(2)}, u32[]{:S(2)}) collective-permute-start(bf16[64,3328]{1,0:T(8,128)(2,1)S(1)} %add_convert_fusion.3), channel_id=1, source_target_pairs={{0,4},{1,1021},{2,6},{3,1023},{4,8},{5,1},{6,10},{7,3},{8,12},{9,5... | collective-permute-start | bytes 1277960 | tf_op jit(solution)/shard_map/ppermute | solution.py:103
  90.0 22.2 %collective-permute-start.10 = (bf16[64,3328]{1,0:T(8,128)(2,1)S(1)}, bf16[64,3328]{1,0:T(8,128)(2,1)S(1)}, u32[]{:S(2)}, u32[]{:S(2)}) collective-permute-start(bf16[64,3328]{1,0:T(8,128)(2,1)S(1)} %add_convert_fusion.2), channel_id=1, source_target_pairs={{0,1020},{1,5},{2,1022},{3,7},{4,0},{5,9},{6,2},{7,11},{8,4},{9,13... | collective-permute-start | bytes 1277960 | tf_op jit(solution)/shard_map/ppermute | solution.py:103
  113.4 16.1 %collective-permute-start.11 = (bf16[64,3328]{1,0:T(8,128)(2,1)S(1)}, bf16[64,3328]{1,0:T(8,128)(2,1)S(1)}, u32[]{:S(2)}, u32[]{:S(2)}) collective-permute-start(bf16[64,3328]{1,0:T(8,128)(2,1)S(1)} %add_convert_fusion.1), channel_id=1, source_target_pairs={{0,2},{1,3},{2,0},{3,1},{4,6},{5,7},{6,4},{7,5},{8,10},{9,11},{10,... | collective-permute-start | bytes 1277960 | tf_op jit(solution)/shard_map/ppermute | solution.py:103
  116.8 3.3 %collective-permute-start.6 = (f32[320,128]{1,0:T(8,128)S(1)}, f32[320,128]{1,0:T(8,128)S(1)}, u32[]{:S(2)}, u32[]{:S(2)}) collective-permute-start(f32[320,128]{1,0:T(8,128)S(1)} %slice.9), channel_id=1, source_target_pairs={{0,1},{1,0},{2,3},{3,2},{4,5},{5,4},{6,7},{7,6},{8,9},{9,8},{10,11... | collective-permute-start | bytes 491528 | tf_op jit(solution)/shard_map/ppermute | solution.py:103

commit v2 on v0

v2 whole, which is shorter than its diff:
```python
import jax
import jax.numpy as jnp
from jax import lax
from jax.experimental import pallas as pl
from jax.experimental.pallas import tpu as pltpu
from jax.sharding import PartitionSpec as P

AXES = ("fsdp", "rep")
HOPS = 2
SPAN = 5
MIB = 1024 * 1024


def _band(near, far, w_own):
    n = near[0].shape[0] // 2
    below = [v[:n] for v in far] + [v[:n] for v in near]
    above = [v[n:] for v in near] + [v[n:] for v in far]
    return jnp.concatenate(below + [w_own[...]] + above, axis=0)


def slope_kernel(with_own, core, tok_a, tok_b, n0, n1, f0, f1, w_own, cot_a, cot_b, p_two, p_one, *rest):
    slope_out, tok_s = rest[-2:]
    rows = w_own.shape[0]
    half = tok_a.shape[1]
    tok_s[:, :half] = tok_a[...]
    tok_s[:, half:] = tok_b[...]
    pre = jnp.dot(tok_s[...].T, _band((n0, n1), (f0, f1), w_own), preferred_element_type=jnp.float32)
    s = 0.5 * jnp.tanh(0.5 * pre) + 0.5
    d = s * (1.0 + pre * (1.0 - s))
    up = jnp.concatenate([cot_a[...], cot_b[...]], axis=0)
    slope = (up.astype(jnp.float32) * d).astype(jnp.bfloat16)
    slope_out[...] = slope[:half]
    two = pl.multiple_of(jnp.where(core[0] == 0, SPAN - 1, 0) * rows, rows)
    one = pl.multiple_of(jnp.where(core[0] == 0, SPAN - 2, 1) * rows, rows)
    blocks = [tok_s[pl.ds(two, rows)], tok_s[pl.ds(one, rows)]]
    if with_own:
        blocks.append(tok_s[HOPS * rows:(HOPS + 1) * rows])
    part = jnp.dot(jnp.concatenate(blocks, axis=0), slope, preferred_element_type=jnp.float32)
    p_two[...] = part[:rows].astype(jnp.bfloat16)
    p_one[...] = part[rows:2 * rows].astype(jnp.bfloat16)
    if with_own:
        rest[0][...] = part[2 * rows:].astype(jnp.bfloat16)


def grad_kernel(core, n0, n1, f0, f1, w_own, s_first, s_second, tg):
    cols = s_first.shape[1]

    def one(first, second):
        band = _band((n0, n1), (f0, f1), w_own)
        total = jnp.zeros(tg.shape, jnp.float32)
        for k, slope in enumerate((first, second)):
            total += lax.dot_general(band[:, k * cols:(k + 1) * cols], slope[...], (((1,), (1,)), ((), ())),
                                     preferred_element_type=jnp.float32)
        tg[...] = total.astype(tg.dtype)

    @pl.when(core[0] == 0)
    def _():
        one(s_second, s_first)

    @pl.when(core[0] != 0)
    def _():
        one(s_first, s_second)


def slopes(core, tok_a, tok_b, pairs, weight, cot_a, cot_b, own_cols):
    width, rows = tok_a.shape
    shard, cols = weight.shape[0], weight.shape[1] // 2
    where = (lambda i, c: (0, c[0])) if own_cols else (lambda i, c: (0, 1 - c[0]))
    whole = lambda v: pl.BlockSpec(v.shape, lambda i, c: (0, 0))
    col = lambda v: pl.BlockSpec((v.shape[0], cols), where)
    out = lambda r: pl.BlockSpec((r, cols), lambda i, c: (0, 0))
    heights = [shard] * (3 if own_cols else 2) + [rows]
    return pl.pallas_call(
        lambda *refs: slope_kernel(own_cols, *refs),
        grid_spec=pltpu.PrefetchScalarGridSpec(
            num_scalar_prefetch=1,
            grid=(1,),
            in_specs=[whole(tok_a), whole(tok_b)] + [col(v) for v in pairs] + [col(weight), col(cot_a), col(cot_b)],
            out_specs=[out(r) for r in heights],
            scratch_shapes=[pltpu.VMEM((width, 2 * rows), jnp.bfloat16)],
        ),
        out_shape=[jax.ShapeDtypeStruct((r, cols), jnp.bfloat16) for r in heights],
        compiler_params=pltpu.CompilerParams(vmem_limit_bytes=40 * MIB),
        cost_estimate=pl.CostEstimate(flops=7 * width * rows * cols, bytes_accessed=6 * MIB,
                                      transcendentals=2 * rows * cols),
    )(core, tok_a, tok_b, *pairs, weight, cot_a, cot_b)


def token_gradient(core, pairs, weight, first, second, width):
    rows = first.shape[0]
    whole = lambda v: pl.BlockSpec(v.shape, lambda i, c: (0, 0))
    return pl.pallas_call(
        grad_kernel,
        grid_spec=pltpu.PrefetchScalarGridSpec(
            num_scalar_prefetch=1,
            grid=(1,),
            in_specs=[whole(v) for v in (*pairs, weight, first, second)],
            out_specs=pl.BlockSpec((width, rows), lambda i, c: (0, 0)),
        ),
        out_shape=jax.ShapeDtypeStruct((width, rows), jnp.bfloat16),
        compiler_params=pltpu.CompilerParams(vmem_limit_bytes=40 * MIB),
        cost_estimate=pl.CostEstimate(flops=4 * width * rows * first.shape[1], bytes_accessed=6 * MIB, transcendentals=0),
    )(core, *pairs, weight, first, second)


def solution(mesh):
    n_f, n_r = mesh.shape["fsdp"], mesh.shape["rep"]

    def pairs_of(move):
        out = []
        for p in range(n_f):
            for r in range(n_r):
                q, t = move(p, r)
                if q != q % n_f:
                    t ^= 2
                out.append((p * n_r + r, (q % n_f) * n_r + t))
        return out

    ring = pairs_of(lambda p, r: (p + (1 if r % 2 == 0 else -1), r))
    swap_core = pairs_of(lambda p, r: (p, r ^ 1))
    swap_far = pairs_of(lambda p, r: (p, r ^ 2))
    core_groups = [[g, g + 1] for g in range(0, n_r, 2)]

    def on_device(tokens, weight, cotangent):
        core = lax.axis_index("rep") % 2
        half = weight.shape[0] // 2

        def send(v, how=ring):
            return lax.ppermute(v, AXES, how)

        def gather(v, axis):
            return lax.all_gather(v, "rep", axis=axis, tiled=True, axis_index_groups=core_groups)

        f32 = lambda v: v.astype(jnp.float32)
        b16 = lambda v: v.astype(jnp.bfloat16)
        near = [send(weight[:half]), send(weight[half:])]
        far = [send(v) for v in near]
        cot_b = send(cotangent, swap_core)
        tok_a = tokens.T
        tok_b = send(tok_a, swap_core)
        pairs = [gather(v, 0) for v in near + far]
        which = core.reshape(1).astype(jnp.int32)
        two, one, slope_1 = slopes(which, tok_a, tok_b, pairs, weight, cotangent, cot_b, False)
        g_1 = send(two)
        two_2, one_2, own, slope_2 = slopes(which, tok_a, tok_b, pairs, weight, cotangent, cot_b, True)
        g_2 = send(two_2)
        g_1 = send(b16(f32(g_1) + f32(one)))
        g_2 = send(b16(f32(g_2) + f32(one_2)))
        got = send(g_1, swap_core)
        mine = b16(f32(own) + f32(g_2) + f32(got))
        other = send(mine, swap_far)
        weight_grad = gather(b16(f32(mine) + f32(other)), 1)
        token_grad = token_gradient(which, pairs, weight, slope_1, slope_2, tokens.shape[1]).T
        return (token_grad, weight_grad)

    return jax.shard_map(
        on_device,
        mesh=mesh,
        in_specs=(P(AXES, None), P("fsdp", None), P(AXES, None)),
        out_specs=(P(AXES, None), P("fsdp", None)),
        check_vma=False,
    )
```

time: 236 us -> 123 us (0.52)
  waiting for transfers between devices: 141 us -> 22.6 us
  starting transfers between devices: 61.6 us -> 78 us
  between operations: 14.2 us -> 0.81 us
  blocking collectives: 0 us -> 12.3 us
  matrix products: 7.51 us -> 0 us
  local copies, waits for them, and re-layouts: 9.98 us -> 2.86 us
  Pallas kernels: 0 us -> 5.54 us
    psum x1 -> x0, waiting for transfers between devices: 64 us -> none  [on_device(): weight_grad = lax.psum(group_grad.astype(jnp.bfloat16), 'rep')]
    ppermute x8 -> x12, waiting for transfers between devices: 76.8 us -> 22.6 us  [send(): return lax.ppermute(v, AXES, how)]
    ppermute x8 -> x12, starting transfers between devices: 61.6 us -> 78 us  [send(): return lax.ppermute(v, AXES, how)]
    all_gather x0 -> x5, blocking collectives: none -> 12.3 us  [gather(): lax.all_gather(v, 'rep', axis=axis, tiled=True, axis_index_groups=core_gr...]
    unnamed x12 -> x7, local copies, waits for them, and re-layouts: 9.65 us -> 0.91 us
    dot_general x3 -> x0, matrix products: 7.51 us -> none  [the longest x1 4.11 us: on_device(): lax.dot_general(slope, stacked, (((1,), (1,)), ((), ())), preferred_eleme...]
    pallas_call x0 -> x3, Pallas kernels: none -> 5.54 us  [the longest x2 3.63 us: slopes(): pl.pallas_call(lambda *refs: slope_kernel(own_cols, *refs), grid_spec=plt...]
  transfers between devices with their start and end apart: 9 -> 12, of which waited for: 8 -> 6; matrix products, arithmetic and copies ran while one was open for 4% -> 2% of each run, Pallas kernels for 0% -> 3%
where the time goes in v2:
time: 123 us
  starting transfers between devices  78 us (63%)
  waiting for transfers between devices  22.6 us (18%)
  blocking collectives  12.3 us (10%)
  Pallas kernels  5.54 us (5%)
  local copies, waits for them, and re-layouts  2.86 us (2%)
    ppermute x12, starting transfers between devices, send(): return lax.ppermute(v, AXES, how)  78 us
    ppermute x12, waiting for transfers between devices, send(): return lax.ppermute(v, AXES, how)  22.6 us
    all_gather x5, blocking collectives, gather(): lax.all_gather(v, 'rep', axis=axis, tiled=True, axis_index_groups=core_gr...  12.3 us
    pallas_call x2, Pallas kernels, slopes(): pl.pallas_call(lambda *refs: slope_kernel(own_cols, *refs), grid_spec=plt...  3.63 us
  transfers between devices with their start and end apart: 12, of which 6 were waited for; matrix products, arithmetic and copies ran while one was open for 2% of the time, Pallas kernels for 3%

profile of v2, /device:TPU:1, one launch (start us, length us, event | category | flops | bytes accessed | tf_op | source)
XLA Modules:
  0.0 122.5 jit_solution(1639285720508468908)
XLA Ops:
  0.6 0.0 copy-start.2
  0.6 16.2 %collective-permute-start.5 = (bf16[128,6656]{1,0:T(8,128)(2,1)}, bf16[128,6656]{1,0:T(8,128)(2,1)S(1)}, u32[]{:S(2)}, u32[]{:S(2)}) collective-permute-start(bf16[128,6656]{1,0:T(8,128)(2,1)} %refs_8_.3), channel_id=1, source_target_pairs={{0,1},{1,0},{2,3},{3,2},{4,5},{5,4},{6,7},{7,6},{8,9},{9,8},{10,11... | collective-permute-start | bytes 5111816 | tf_op jit(solution)/shard_map/ppermute | solution.py:129
  16.8 2.0 %fusion = (bf16[32,6656]{1,0:T(8,128)(2,1)S(1)}, bf16[32,6656]{1,0:T(8,128)(2,1)}) fusion(bf16[64,6656]{1,0:T(8,128)(2,1)} %w_own.1), kind=kLoop, calls=%fused_computation.4 | loop fusion | bytes 1703936 | tf_op jit(solution)/shard_map/slice | solution.py:136
  18.8 10.4 %collective-permute-start = (bf16[32,6656]{1,0:T(8,128)(2,1)}, bf16[32,6656]{1,0:T(8,128)(2,1)S(1)}, u32[]{:S(2)}, u32[]{:S(2)}) collective-permute-start(bf16[32,6656]{1,0:T(8,128)(2,1)} %get-tuple-element.17), channel_id=1, source_target_pairs={{0,4},{1,1023},{2,6},{3,1021},{4,8},{5,1},{6,10},{7,3},{8,12},{9,5... | collective-permute-start | bytes 1277960 | tf_op jit(solution)/shard_map/ppermute | solution.py:129
  29.2 2.2 %collective-permute-start.1 = (bf16[32,6656]{1,0:T(8,128)(2,1)S(1)}, bf16[32,6656]{1,0:T(8,128)(2,1)S(1)}, u32[]{:S(2)}, u32[]{:S(2)}) collective-permute-start(bf16[32,6656]{1,0:T(8,128)(2,1)S(1)} %get-tuple-element.16), channel_id=1, source_target_pairs={{0,4},{1,1023},{2,6},{3,1021},{4,8},{5,1},{6,10},{7,3},{8,12},{9,5... | collective-permute-start | bytes 1277960 | tf_op jit(solution)/shard_map/ppermute | solution.py:129
  31.4 0.0 copy-done.2
  31.4 1.9 %collective-permute-start.4 = (bf16[320,128]{1,0:T(8,128)(2,1)S(1)}, bf16[320,128]{1,0:T(8,128)(2,1)S(1)}, u32[]{:S(2)}, u32[]{:S(2)}) collective-permute-start(bf16[320,128]{1,0:T(8,128)(2,1)S(1)} %bitcast.3), channel_id=1, source_target_pairs={{0,1},{1,0},{2,3},{3,2},{4,5},{5,4},{6,7},{7,6},{8,9},{9,8},{10,11... | collective-permute-start | bytes 245768 | tf_op jit(solution)/shard_map/ppermute | solution.py:129
  33.3 1.2 %collective-permute-done = bf16[32,6656]{1,0:T(8,128)(2,1)S(1)} collective-permute-done((bf16[32,6656]{1,0:T(8,128)(2,1)}, bf16[32,6656]{1,0:T(8,128)(2,1)S(1)}, u32[]{:S(2)}, u32[]{:S(2)}) %collective-permute-start) | collective-permute-done | bytes 426016 | tf_op jit(solution)/shard_map/ppermute | solution.py:129
  34.6 9.1 %collective-permute-start.2 = (bf16[32,6656]{1,0:T(8,128)(2,1)S(1)}, bf16[32,6656]{1,0:T(8,128)(2,1)S(1)}, u32[]{:S(2)}, u32[]{:S(2)}) collective-permute-start(bf16[32,6656]{1,0:T(8,128)(2,1)S(1)} %collective-permute-done), channel_id=1, source_target_pairs={{0,4},{1,1023},{2,6},{3,1021},{4,8},{5,1},{6,10},{7,3},{8,12},{9,5... | collective-permute-start | bytes 1277960 | tf_op jit(solution)/shard_map/ppermute | solution.py:129
  43.7 0.0 collective-permute-done.1
  43.7 4.5 %collective-permute-start.3 = (bf16[32,6656]{1,0:T(8,128)(2,1)S(1)}, bf16[32,6656]{1,0:T(8,128)(2,1)S(1)}, u32[]{:S(2)}, u32[]{:S(2)}) collective-permute-start(bf16[32,6656]{1,0:T(8,128)(2,1)S(1)} %collective-permute-done.1), channel_id=1, source_target_pairs={{0,4},{1,1023},{2,6},{3,1021},{4,8},{5,1},{6,10},{7,3},{8,12},{9,5... | collective-permute-start | bytes 1277960 | tf_op jit(solution)/shard_map/ppermute | solution.py:129
  48.2 2.4 %all_gather.15.refs_3_.n0 = bf16[64,6656]{1,0:T(8,128)(2,1)S(1)} all-gather(bf16[32,6656]{1,0:T(8,128)(2,1)S(1)} %collective-permute-done), channel_id=1, replica_groups={{0,1},{2,3},{4,5},{6,7},{8,9},{10,11},{12,13},{14,15},{16,17},{18,19},{..., dimensions={0}, use_global_device_ids=true | all-gather | bytes 1277952 | tf_op jit(solution)/shard_map/all_gather | solution.py:132
  50.7 0.0 copy-start
  50.7 0.0 copy-start.1
  50.7 2.5 %all_gather.16.refs_4_.n1 = bf16[64,6656]{1,0:T(8,128)(2,1)S(1)} all-gather(bf16[32,6656]{1,0:T(8,128)(2,1)S(1)} %collective-permute-done.1), channel_id=1, replica_groups={{0,1},{2,3},{4,5},{6,7},{8,9},{10,11},{12,13},{14,15},{16,17},{18,19},{..., dimensions={0}, use_global_device_ids=true | all-gather | bytes 1277952 | tf_op jit(solution)/shard_map/all_gather | solution.py:132
  53.2 0.0 collective-permute-done.2
  53.2 2.4 %all_gather.17.refs_5_.f0 = bf16[64,6656]{1,0:T(8,128)(2,1)S(1)} all-gather(bf16[32,6656]{1,0:T(8,128)(2,1)S(1)} %collective-permute-done.2), channel_id=1, replica_groups={{0,1},{2,3},{4,5},{6,7},{8,9},{10,11},{12,13},{14,15},{16,17},{18,19},{..., dimensions={0}, use_global_device_ids=true | all-gather | bytes 1277952 | tf_op jit(solution)/shard_map/all_gather | solution.py:132
  55.6 0.0 collective-permute-done.3
  55.6 2.4 %all_gather.18.refs_6_.f1 = bf16[64,6656]{1,0:T(8,128)(2,1)S(1)} all-gather(bf16[32,6656]{1,0:T(8,128)(2,1)S(1)} %collective-permute-done.3), channel_id=1, replica_groups={{0,1},{2,3},{4,5},{6,7},{8,9},{10,11},{12,13},{14,15},{16,17},{18,19},{..., dimensions={0}, use_global_device_ids=true | all-gather | bytes 1277952 | tf_op jit(solution)/shard_map/all_gather | solution.py:132
  58.0 0.0 collective-permute-done.4.refs_2_
  58.0 0.0 collective-permute-done.5.refs_9_
  58.0 0.0 copy-done
  58.0 0.0 copy-done.1
  58.0 1.8 %shard_map.50 = (bf16[64,3328]{1,0:T(8,128)(2,1)S(1)}, bf16[64,3328]{1,0:T(8,128)(2,1)S(1)}, bf16[128,3328]{1,0:T(8,128)(2,1)S(1)}) custom-call(s32[1]{0:T(128)} %bitcast.refs_0_.core, bf16[320,128]{1,0:T(8,128)(2,1)S(1)} %bitcast.4, bf16[320,128]{1,0:T(8,128)(2,1)S(1)} %collective-permute-done.4.refs_2_, bf16[64,6656]{1,0:T(8,128)(2,1)S(1)} %all_gather.15.refs_3_.n0, ...), custom_call_target="tpu_custom_call" | custom-call | flops 954204160 | bytes 6291456 | tf_op jit(solution)/shard_map/pallas_call | solution.py:73
  59.8 6.9 %collective-permute-start.8 = (bf16[64,3328]{1,0:T(8,128)(2,1)S(1)}, bf16[64,3328]{1,0:T(8,128)(2,1)S(1)}, u32[]{:S(2)}, u32[]{:S(2)}) collective-permute-start(bf16[64,3328]{1,0:T(8,128)(2,1)S(1)} %get-tuple-element.14), channel_id=1, source_target_pairs={{0,4},{1,1023},{2,6},{3,1021},{4,8},{5,1},{6,10},{7,3},{8,12},{9,5... | collective-permute-start | bytes 1277960 | tf_op jit(solution)/shard_map/ppermute | solution.py:129
  66.8 1.9 %shard_map.51 = (bf16[64,3328]{1,0:T(8,128)(2,1)S(1)}, bf16[64,3328]{1,0:T(8,128)(2,1)S(1)}, bf16[64,3328]{1,0:T(8,128)(2,1)S(1)}, bf16[128,3328]{1,0:T(8,128)(2,1)S(1)}) custom-call(s32[1]{0:T(128)} %bitcast.refs_0_.core, bf16[320,128]{1,0:T(8,128)(2,1)S(1)} %bitcast.5, bf16[320,128]{1,0:T(8,128)(2,1)S(1)} %collective-permute-done.4.refs_2_, ...), custom_call_target="tpu_custom_call" | custom-call | flops 954204160 | bytes 6291456 | tf_op jit(solution)/shard_map/pallas_call | solution.py:73
  68.6 1.9 %collective-permute-start.6 = (bf16[64,3328]{1,0:T(8,128)(2,1)S(1)}, bf16[64,3328]{1,0:T(8,128)(2,1)S(1)}, u32[]{:S(2)}, u32[]{:S(2)}) collective-permute-start(bf16[64,3328]{1,0:T(8,128)(2,1)S(1)} %get-tuple-element.12), channel_id=1, source_target_pairs={{0,4},{1,1023},{2,6},{3,1021},{4,8},{5,1},{6,10},{7,3},{8,12},{9,5... | collective-permute-start | bytes 1277960 | tf_op jit(solution)/shard_map/ppermute | solution.py:129
  70.5 1.3 %collective-permute-done.8 = bf16[64,3328]{1,0:T(8,128)(2,1)S(1)} collective-permute-done((bf16[64,3328]{1,0:T(8,128)(2,1)S(1)}, bf16[64,3328]{1,0:T(8,128)(2,1)S(1)}, u32[]{:S(2)}, u32[]{:S(2)}) %collective-permute-start.8) | collective-permute-done | bytes 426016 | tf_op jit(solution)/shard_map/ppermute | solution.py:129
  71.8 0.1 add_convert_fusion.2
  71.9 9.2 %collective-permute-start.9 = (bf16[64,3328]{1,0:T(8,128)(2,1)S(1)}, bf16[64,3328]{1,0:T(8,128)(2,1)S(1)}, u32[]{:S(2)}, u32[]{:S(2)}) collective-permute-start(bf16[64,3328]{1,0:T(8,128)(2,1)S(1)} %add_convert_fusion.2), channel_id=1, source_target_pairs={{0,4},{1,1023},{2,6},{3,1021},{4,8},{5,1},{6,10},{7,3},{8,12},{9,5... | collective-permute-start | bytes 1277960 | tf_op jit(solution)/shard_map/ppermute | solution.py:129
  81.2 0.0 collective-permute-done.6
  81.2 0.1 add_convert_fusion.3
  81.3 4.4 %collective-permute-start.7 = (bf16[64,3328]{1,0:T(8,128)(2,1)S(1)}, bf16[64,3328]{1,0:T(8,128)(2,1)S(1)}, u32[]{:S(2)}, u32[]{:S(2)}) collective-permute-start(bf16[64,3328]{1,0:T(8,128)(2,1)S(1)} %add_convert_fusion.3), channel_id=1, source_target_pairs={{0,4},{1,1023},{2,6},{3,1021},{4,8},{5,1},{6,10},{7,3},{8,12},{9,5... | collective-permute-start | bytes 1277960 | tf_op jit(solution)/shard_map/ppermute | solution.py:129
  85.7 0.5 collective-permute-done.9
  86.2 6.7 %collective-permute-start.10 = (bf16[64,3328]{1,0:T(8,128)(2,1)S(1)}, bf16[64,3328]{1,0:T(8,128)(2,1)S(1)}, u32[]{:S(2)}, u32[]{:S(2)}) collective-permute-start(bf16[64,3328]{1,0:T(8,128)(2,1)S(1)} %collective-permute-done.9), channel_id=1, source_target_pairs={{0,1},{1,0},{2,3},{3,2},{4,5},{5,4},{6,7},{7,6},{8,9},{9,8},{10,11... | collective-permute-start | bytes 1277960 | tf_op jit(solution)/shard_map/ppermute | solution.py:129
  92.9 0.5 collective-permute-done.7
  93.4 0.9 collective-permute-done.10
  94.2 0.2 add_convert_fusion.1
  94.4 4.4 %collective-permute-start.11 = (bf16[64,3328]{1,0:T(8,128)(2,1)S(1)}, bf16[64,3328]{1,0:T(8,128)(2,1)S(1)}, u32[]{:S(2)}, u32[]{:S(2)}) collective-permute-start(bf16[64,3328]{1,0:T(8,128)(2,1)S(1)} %add_convert_fusion.1), channel_id=1, source_target_pairs={{0,2},{1,3},{2,0},{3,1},{4,6},{5,7},{6,4},{7,5},{8,10},{9,11},{10,... | collective-permute-start | bytes 1277960 | tf_op jit(solution)/shard_map/ppermute | solution.py:129
  98.8 1.9 %shard_map.52 = bf16[320,128]{1,0:T(8,128)(2,1)} custom-call(s32[1]{0:T(128)} %bitcast.refs_0_.core, bf16[64,6656]{1,0:T(8,128)(2,1)S(1)} %all_gather.15.refs_3_.n0, bf16[64,6656]{1,0:T(8,128)(2,1)S(1)} %all_gather.16.refs_4_.n1, bf16[64,6656]{1,0:T(8,128)(2,1)S(1)} %all_gather.17.refs_5_.f0, bf16[64,6656]{1,0:T(8,128)(2,1)S(1)} %all_gather.18.refs_6_.f1, ...), custom_call_target="tpu_custom_call" | custom-call | flops 545259520 | bytes 6291456 | tf_op jit(solution)/shard_map/pallas_call | solution.py:92
  100.8 18.3 %collective-permute-done.11 = bf16[64,3328]{1,0:T(8,128)(2,1)S(1)} collective-permute-done((bf16[64,3328]{1,0:T(8,128)(2,1)S(1)}, bf16[64,3328]{1,0:T(8,128)(2,1)S(1)}, u32[]{:S(2)}, u32[]{:S(2)}) %collective-permute-start.11) | collective-permute-done | bytes 426016 | tf_op jit(solution)/shard_map/ppermute | solution.py:129
  119.0 0.1 add_convert_fusion
  119.1 2.5 %all_gather.19 = bf16[64,6656]{1,0:T(8,128)(2,1)S(1)} all-gather(bf16[64,3328]{1,0:T(8,128)(2,1)S(1)} %add_convert_fusion), channel_id=1, replica_groups={{0,1},{2,3},{4,5},{6,7},{8,9},{10,11},{12,13},{14,15},{16,17},{18,19},{..., dimensions={1}, use_global_device_ids=true | all-gather | bytes 1277952 | tf_op jit(solution)/shard_map/all_gather | solution.py:132
  121.6 0.9 copy.6
Async XLA Ops:
  0.6 30.7 %copy-start.2 = (bf16[128,320]{0,1:T(8,128)(2,1)S(1)}, bf16[128,320]{0,1:T(8,128)(2,1)}, u32[]{:S(2)}) copy-start(bf16[128,320]{0,1:T(8,128)(2,1)} %param.3) | copy-start | bytes 245764
  0.6 57.4 %collective-permute-start.5 = (bf16[128,6656]{1,0:T(8,128)(2,1)}, bf16[128,6656]{1,0:T(8,128)(2,1)S(1)}, u32[]{:S(2)}, u32[]{:S(2)}) collective-permute-start(bf16[128,6656]{1,0:T(8,128)(2,1)} %refs_8_.3), channel_id=1, source_target_pairs={{0,1},{1,0},{2,3},{3,2},{4,5},{5,4},{6,7},{7,6},{8,9},{9,8},{10,11... | collective-permute-start | bytes 5111816 | tf_op jit(solution)/shard_map/ppermute | solution.py:129
  18.8 15.8 %collective-permute-start = (bf16[32,6656]{1,0:T(8,128)(2,1)}, bf16[32,6656]{1,0:T(8,128)(2,1)S(1)}, u32[]{:S(2)}, u32[]{:S(2)}) collective-permute-start(bf16[32,6656]{1,0:T(8,128)(2,1)} %get-tuple-element.17), channel_id=1, source_target_pairs={{0,4},{1,1023},{2,6},{3,1021},{4,8},{5,1},{6,10},{7,3},{8,12},{9,5... | collective-permute-start | bytes 1277960 | tf_op jit(solution)/shard_map/ppermute | solution.py:129
  29.2 14.5 %collective-permute-start.1 = (bf16[32,6656]{1,0:T(8,128)(2,1)S(1)}, bf16[32,6656]{1,0:T(8,128)(2,1)S(1)}, u32[]{:S(2)}, u32[]{:S(2)}) collective-permute-start(bf16[32,6656]{1,0:T(8,128)(2,1)S(1)} %get-tuple-element.16), channel_id=1, source_target_pairs={{0,4},{1,1023},{2,6},{3,1021},{4,8},{5,1},{6,10},{7,3},{8,12},{9,5... | collective-permute-start | bytes 1277960 | tf_op jit(solution)/shard_map/ppermute | solution.py:129
  31.4 26.6 %collective-permute-start.4 = (bf16[320,128]{1,0:T(8,128)(2,1)S(1)}, bf16[320,128]{1,0:T(8,128)(2,1)S(1)}, u32[]{:S(2)}, u32[]{:S(2)}) collective-permute-start(bf16[320,128]{1,0:T(8,128)(2,1)S(1)} %bitcast.3), channel_id=1, source_target_pairs={{0,1},{1,0},{2,3},{3,2},{4,5},{5,4},{6,7},{7,6},{8,9},{9,8},{10,11... | collective-permute-start | bytes 245768 | tf_op jit(solution)/shard_map/ppermute | solution.py:129
  34.6 18.7 %collective-permute-start.2 = (bf16[32,6656]{1,0:T(8,128)(2,1)S(1)}, bf16[32,6656]{1,0:T(8,128)(2,1)S(1)}, u32[]{:S(2)}, u32[]{:S(2)}) collective-permute-start(bf16[32,6656]{1,0:T(8,128)(2,1)S(1)} %collective-permute-done), channel_id=1, source_target_pairs={{0,4},{1,1023},{2,6},{3,1021},{4,8},{5,1},{6,10},{7,3},{8,12},{9,5... | collective-permute-start | bytes 1277960 | tf_op jit(solution)/shard_map/ppermute | solution.py:129
  43.7 11.9 %collective-permute-start.3 = (bf16[32,6656]{1,0:T(8,128)(2,1)S(1)}, bf16[32,6656]{1,0:T(8,128)(2,1)S(1)}, u32[]{:S(2)}, u32[]{:S(2)}) collective-permute-start(bf16[32,6656]{1,0:T(8,128)(2,1)S(1)} %collective-permute-done.1), channel_id=1, source_target_pairs={{0,4},{1,1023},{2,6},{3,1021},{4,8},{5,1},{6,10},{7,3},{8,12},{9,5... | collective-permute-start | bytes 1277960 | tf_op jit(solution)/shard_map/ppermute | solution.py:129
  50.7 7.4 %copy-start = (bf16[64,6656]{1,0:T(8,128)(2,1)S(1)}, bf16[64,6656]{1,0:T(8,128)(2,1)}, u32[]{:S(2)}) copy-start(bf16[64,6656]{1,0:T(8,128)(2,1)} %w_own.1) | copy-start | bytes 2555908
  50.7 7.4 %copy-start.1 = (bf16[128,6656]{1,0:T(8,128)(2,1)S(1)}, bf16[128,6656]{1,0:T(8,128)(2,1)}, u32[]{:S(2)}) copy-start(bf16[128,6656]{1,0:T(8,128)(2,1)} %refs_8_.3) | copy-start | bytes 5111812
  59.8 12.0 %collective-permute-start.8 = (bf16[64,3328]{1,0:T(8,128)(2,1)S(1)}, bf16[64,3328]{1,0:T(8,128)(2,1)S(1)}, u32[]{:S(2)}, u32[]{:S(2)}) collective-permute-start(bf16[64,3328]{1,0:T(8,128)(2,1)S(1)} %get-tuple-element.14), channel_id=1, source_target_pairs={{0,4},{1,1023},{2,6},{3,1021},{4,8},{5,1},{6,10},{7,3},{8,12},{9,5... | collective-permute-start | bytes 1277960 | tf_op jit(solution)/shard_map/ppermute | solution.py:129
  68.6 12.5 %collective-permute-start.6 = (bf16[64,3328]{1,0:T(8,128)(2,1)S(1)}, bf16[64,3328]{1,0:T(8,128)(2,1)S(1)}, u32[]{:S(2)}, u32[]{:S(2)}) collective-permute-start(bf16[64,3328]{1,0:T(8,128)(2,1)S(1)} %get-tuple-element.12), channel_id=1, source_target_pairs={{0,4},{1,1023},{2,6},{3,1021},{4,8},{5,1},{6,10},{7,3},{8,12},{9,5... | collective-permute-start | bytes 1277960 | tf_op jit(solution)/shard_map/ppermute | solution.py:129
  71.9 14.3 %collective-permute-start.9 = (bf16[64,3328]{1,0:T(8,128)(2,1)S(1)}, bf16[64,3328]{1,0:T(8,128)(2,1)S(1)}, u32[]{:S(2)}, u32[]{:S(2)}) collective-permute-start(bf16[64,3328]{1,0:T(8,128)(2,1)S(1)} %add_convert_fusion.2), channel_id=1, source_target_pairs={{0,4},{1,1023},{2,6},{3,1021},{4,8},{5,1},{6,10},{7,3},{8,12},{9,5... | collective-permute-start | bytes 1277960 | tf_op jit(solution)/shard_map/ppermute | solution.py:129
  81.3 12.1 %collective-permute-start.7 = (bf16[64,3328]{1,0:T(8,128)(2,1)S(1)}, bf16[64,3328]{1,0:T(8,128)(2,1)S(1)}, u32[]{:S(2)}, u32[]{:S(2)}) collective-permute-start(bf16[64,3328]{1,0:T(8,128)(2,1)S(1)} %add_convert_fusion.3), channel_id=1, source_target_pairs={{0,4},{1,1023},{2,6},{3,1021},{4,8},{5,1},{6,10},{7,3},{8,12},{9,5... | collective-permute-start | bytes 1277960 | tf_op jit(solution)/shard_map/ppermute | solution.py:129
  86.2 8.0 %collective-permute-start.10 = (bf16[64,3328]{1,0:T(8,128)(2,1)S(1)}, bf16[64,3328]{1,0:T(8,128)(2,1)S(1)}, u32[]{:S(2)}, u32[]{:S(2)}) collective-permute-start(bf16[64,3328]{1,0:T(8,128)(2,1)S(1)} %collective-permute-done.9), channel_id=1, source_target_pairs={{0,1},{1,0},{2,3},{3,2},{4,5},{5,4},{6,7},{7,6},{8,9},{9,8},{10,11... | collective-permute-start | bytes 1277960 | tf_op jit(solution)/shard_map/ppermute | solution.py:129
  94.4 24.6 %collective-permute-start.11 = (bf16[64,3328]{1,0:T(8,128)(2,1)S(1)}, bf16[64,3328]{1,0:T(8,128)(2,1)S(1)}, u32[]{:S(2)}, u32[]{:S(2)}) collective-permute-start(bf16[64,3328]{1,0:T(8,128)(2,1)S(1)} %add_convert_fusion.1), channel_id=1, source_target_pairs={{0,2},{1,3},{2,0},{3,1},{4,6},{5,7},{6,4},{7,5},{8,10},{9,11},{10,... | collective-permute-start | bytes 1277960 | tf_op jit(solution)/shard_map/ppermute | solution.py:129

commit v3 on v2

--- a/solution.py
+++ b/solution.py
@@ -7,6 +7,7 @@
 
 AXES = ("fsdp", "rep")
 HOPS = 2
+LINE = 16
 SPAN = 5
 MIB = 1024 * 1024
 
@@ -117,6 +118,9 @@
         return out
 
     ring = pairs_of(lambda p, r: (p + (1 if r % 2 == 0 else -1), r))
+    crosses = lambda pair: (pair[0] // n_r) // LINE != (pair[1] // n_r) // LINE
+    inner = [pair for pair in ring if not crosses(pair)]
+    outer = [pair for pair in ring if crosses(pair)]
     swap_core = pairs_of(lambda p, r: (p, r ^ 1))
     swap_far = pairs_of(lambda p, r: (p, r ^ 2))
     core_groups = [[g, g + 1] for g in range(0, n_r, 2)]
@@ -125,7 +129,7 @@
         core = lax.axis_index("rep") % 2
         half = weight.shape[0] // 2
 
-        def send(v, how=ring):
+        def send(v, how):
             return lax.ppermute(v, AXES, how)
 
         def gather(v, axis):
@@ -133,19 +137,24 @@
 
         f32 = lambda v: v.astype(jnp.float32)
         b16 = lambda v: v.astype(jnp.bfloat16)
-        near = [send(weight[:half]), send(weight[half:])]
-        far = [send(v) for v in near]
+        step_in = send(weight, inner)
+        step_out = send(weight, outer)
+        far_out = send(step_in, outer)
+        step = step_in + step_out
+        near = [step[:half], step[half:]]
+        far = [send(v, inner) for v in near]
+        far = [far[0] + far_out[:half], far[1] + far_out[half:]]
         cot_b = send(cotangent, swap_core)
         tok_a = tokens.T
         tok_b = send(tok_a, swap_core)
         pairs = [gather(v, 0) for v in near + far]
         which = core.reshape(1).astype(jnp.int32)
         two, one, slope_1 = slopes(which, tok_a, tok_b, pairs, weight, cotangent, cot_b, False)
-        g_1 = send(two)
+        g_1 = send(two, ring)
         two_2, one_2, own, slope_2 = slopes(which, tok_a, tok_b, pairs, weight, cotangent, cot_b, True)
-        g_2 = send(two_2)
-        g_1 = send(b16(f32(g_1) + f32(one)))
-        g_2 = send(b16(f32(g_2) + f32(one_2)))
+        g_2 = send(two_2, ring)
+        g_1 = send(b16(f32(g_1) + f32(one)), ring)
+        g_2 = send(b16(f32(g_2) + f32(one_2)), ring)
         got = send(g_1, swap_core)
         mine = b16(f32(own) + f32(g_2) + f32(got))
         other = send(mine, swap_far)

time: 123 us -> 122 us (level)
  starting transfers between devices: 78 us -> 74.1 us
  waiting for transfers between devices: 22.6 us -> 26.5 us
  local copies, waits for them, and re-layouts: 2.86 us -> 0.97 us
    ppermute x12 -> x13, waiting for transfers between devices: 22.6 us -> 26.5 us  [send(): return lax.ppermute(v, AXES, how)]
    ppermute x12 -> x13, starting transfers between devices: 78 us -> 74.1 us  [send(): return lax.ppermute(v, AXES, how)]
    slice x1, local copies, waits for them, and re-layouts: 1.95 us -> 0.06 us  [on_device(): near = [step[:half], step[half:]]]
  transfers between devices with their start and end apart: 12 -> 13, of which waited for: 6 -> 4; matrix products, arithmetic and copies ran while one was open for 2% -> 0% of each run, Pallas kernels for 3% -> 3%
where the time goes in v3:
time: 122 us; the launch traced here: 121 us
  starting transfers between devices  74.1 us (61%)
  waiting for transfers between devices  26.5 us (22%)
  blocking collectives  12.4 us (10%)
  Pallas kernels  5.54 us (5%)
    ppermute x13, starting transfers between devices, send(): return lax.ppermute(v, AXES, how)  74.1 us
    ppermute x13, waiting for transfers between devices, send(): return lax.ppermute(v, AXES, how)  26.5 us
    all_gather x5, blocking collectives, gather(): lax.all_gather(v, 'rep', axis=axis, tiled=True, axis_index_groups=core_gr...  12.4 us
    pallas_call x2, Pallas kernels, slopes(): pl.pallas_call(lambda *refs: slope_kernel(own_cols, *refs), grid_spec=plt...  3.63 us
  transfers between devices with their start and end apart: 13, of which 4 were waited for; matrix products, arithmetic and copies ran while one was open for 0% of the time, Pallas kernels for 3%

profile of v3, /device:TPU:1, one launch (start us, length us, event | category | flops | bytes accessed | tf_op | source)
XLA Modules:
  0.0 121.2 jit_solution(14373045966370535243)
XLA Ops:
  0.6 1.3 %collective-permute-start = (bf16[64,6656]{1,0:T(8,128)(2,1)}, bf16[64,6656]{1,0:T(8,128)(2,1)S(1)}, u32[]{:S(2)}, u32[]{:S(2)}) collective-permute-start(bf16[64,6656]{1,0:T(8,128)(2,1)} %w_own.1), channel_id=1, source_target_pairs={{0,4},{2,6},{4,8},{5,1},{6,10},{7,3},{8,12},{9,5},{10,14},{11,7},{... | collective-permute-start | bytes 2555912 | tf_op jit(solution)/shard_map/ppermute | solution.py:133
  1.9 24.9 %collective-permute-start.1 = (bf16[64,6656]{1,0:T(8,128)(2,1)}, bf16[64,6656]{1,0:T(8,128)(2,1)S(1)}, u32[]{:S(2)}, u32[]{:S(2)}) collective-permute-start(bf16[64,6656]{1,0:T(8,128)(2,1)} %w_own.1), channel_id=1, source_target_pairs={{1,1023},{3,1021},{60,64},{62,66},{65,61},{67,63},{124,128},{126,1... | collective-permute-start | bytes 2555912 | tf_op jit(solution)/shard_map/ppermute | solution.py:133
  26.8 1.9 %collective-permute-start.5 = (bf16[320,128]{1,0:T(8,128)(2,1)}, bf16[320,128]{1,0:T(8,128)(2,1)S(1)}, u32[]{:S(2)}, u32[]{:S(2)}) collective-permute-start(bf16[320,128]{1,0:T(8,128)(2,1)} %bitcast.3), channel_id=1, source_target_pairs={{0,1},{1,0},{2,3},{3,2},{4,5},{5,4},{6,7},{7,6},{8,9},{9,8},{10,11... | collective-permute-start | bytes 245768 | tf_op jit(solution)/shard_map/ppermute | solution.py:133
  28.7 2.4 %collective-permute-start.6 = (bf16[128,6656]{1,0:T(8,128)(2,1)}, bf16[128,6656]{1,0:T(8,128)(2,1)S(1)}, u32[]{:S(2)}, u32[]{:S(2)}) collective-permute-start(bf16[128,6656]{1,0:T(8,128)(2,1)} %refs_8_.3), channel_id=1, source_target_pairs={{0,1},{1,0},{2,3},{3,2},{4,5},{5,4},{6,7},{7,6},{8,9},{9,8},{10,11... | collective-permute-start | bytes 5111816 | tf_op jit(solution)/shard_map/ppermute | solution.py:133
  31.2 0.0 collective-permute-done
  31.2 5.5 %collective-permute-start.3 = (bf16[64,6656]{1,0:T(8,128)(2,1)S(1)}, bf16[64,6656]{1,0:T(8,128)(2,1)S(1)}, u32[]{:S(2)}, u32[]{:S(2)}) collective-permute-start(bf16[64,6656]{1,0:T(8,128)(2,1)S(1)} %collective-permute-done), channel_id=1, source_target_pairs={{1,1023},{3,1021},{60,64},{62,66},{65,61},{67,63},{124,128},{126,1... | collective-permute-start | bytes 2555912 | tf_op jit(solution)/shard_map/ppermute | solution.py:133
  36.7 0.0 collective-permute-done.1
  36.7 0.2 add.29
  36.9 0.1 fusion
  36.9 1.3 %collective-permute-start.2 = (bf16[32,6656]{1,0:T(8,128)(2,1)S(1)}, bf16[32,6656]{1,0:T(8,128)(2,1)S(1)}, u32[]{:S(2)}, u32[]{:S(2)}) collective-permute-start(bf16[32,6656]{1,0:T(8,128)(2,1)S(1)} %get-tuple-element.19), channel_id=1, source_target_pairs={{0,4},{2,6},{4,8},{5,1},{6,10},{7,3},{8,12},{9,5},{10,14},{11,7},{... | collective-permute-start | bytes 1277960 | tf_op jit(solution)/shard_map/ppermute | solution.py:133
  38.2 1.3 %collective-permute-start.4 = (bf16[32,6656]{1,0:T(8,128)(2,1)S(1)}, bf16[32,6656]{1,0:T(8,128)(2,1)S(1)}, u32[]{:S(2)}, u32[]{:S(2)}) collective-permute-start(bf16[32,6656]{1,0:T(8,128)(2,1)S(1)} %get-tuple-element.18), channel_id=1, source_target_pairs={{0,4},{2,6},{4,8},{5,1},{6,10},{7,3},{8,12},{9,5},{10,14},{11,7},{... | collective-permute-start | bytes 1277960 | tf_op jit(solution)/shard_map/ppermute | solution.py:133
  39.5 2.4 %all_gather.15.refs_3_.n0 = bf16[64,6656]{1,0:T(8,128)(2,1)S(1)} all-gather(bf16[32,6656]{1,0:T(8,128)(2,1)S(1)} %get-tuple-element.19), channel_id=1, replica_groups={{0,1},{2,3},{4,5},{6,7},{8,9},{10,11},{12,13},{14,15},{16,17},{18,19},{..., dimensions={0}, use_global_device_ids=true | all-gather | bytes 1277952 | tf_op jit(solution)/shard_map/all_gather | solution.py:136
  42.0 2.4 %all_gather.16.refs_4_.n1 = bf16[64,6656]{1,0:T(8,128)(2,1)S(1)} all-gather(bf16[32,6656]{1,0:T(8,128)(2,1)S(1)} %get-tuple-element.18), channel_id=1, replica_groups={{0,1},{2,3},{4,5},{6,7},{8,9},{10,11},{12,13},{14,15},{16,17},{18,19},{..., dimensions={0}, use_global_device_ids=true | all-gather | bytes 1277952 | tf_op jit(solution)/shard_map/all_gather | solution.py:136
  44.4 1.7 %collective-permute-done.2 = bf16[32,6656]{1,0:T(8,128)(2,1)S(1)} collective-permute-done((bf16[32,6656]{1,0:T(8,128)(2,1)S(1)}, bf16[32,6656]{1,0:T(8,128)(2,1)S(1)}, u32[]{:S(2)}, u32[]{:S(2)}) %collective-permute-start.2) | collective-permute-done | bytes 426016 | tf_op jit(solution)/shard_map/ppermute | solution.py:133
  46.1 4.6 %collective-permute-done.4 = bf16[32,6656]{1,0:T(8,128)(2,1)S(1)} collective-permute-done((bf16[32,6656]{1,0:T(8,128)(2,1)S(1)}, bf16[32,6656]{1,0:T(8,128)(2,1)S(1)}, u32[]{:S(2)}, u32[]{:S(2)}) %collective-permute-start.4) | collective-permute-done | bytes 426016 | tf_op jit(solution)/shard_map/ppermute | solution.py:133
  50.7 0.0 collective-permute-done.3
  50.7 0.0 copy-start.2
  50.7 0.1 slice_add_fusion
  50.8 0.0 copy-start
  50.8 0.0 copy-start.1
  50.8 2.7 %all_gather.17.refs_5_.f0 = bf16[64,6656]{1,0:T(8,128)(2,1)S(1)} all-gather(bf16[32,6656]{1,0:T(8,128)(2,1)S(1)} %get-tuple-element.17), channel_id=1, replica_groups={{0,1},{2,3},{4,5},{6,7},{8,9},{10,11},{12,13},{14,15},{16,17},{18,19},{..., dimensions={0}, use_global_device_ids=true | all-gather | bytes 1277952 | tf_op jit(solution)/shard_map/all_gather | solution.py:136
  53.5 2.4 %all_gather.18.refs_6_.f1 = bf16[64,6656]{1,0:T(8,128)(2,1)S(1)} all-gather(bf16[32,6656]{1,0:T(8,128)(2,1)S(1)} %get-tuple-element.16), channel_id=1, replica_groups={{0,1},{2,3},{4,5},{6,7},{8,9},{10,11},{12,13},{14,15},{16,17},{18,19},{..., dimensions={0}, use_global_device_ids=true | all-gather | bytes 1277952 | tf_op jit(solution)/shard_map/all_gather | solution.py:136
  55.9 0.0 collective-permute-done.5.refs_2_
  55.9 0.0 collective-permute-done.6.refs_9_
  55.9 0.0 copy-done.2
  55.9 0.0 copy-done
  55.9 0.0 copy-done.1
  55.9 1.8 %shard_map.50 = (bf16[64,3328]{1,0:T(8,128)(2,1)S(1)}, bf16[64,3328]{1,0:T(8,128)(2,1)S(1)}, bf16[128,3328]{1,0:T(8,128)(2,1)S(1)}) custom-call(s32[1]{0:T(128)} %bitcast.refs_0_.core, bf16[320,128]{1,0:T(8,128)(2,1)S(1)} %bitcast.4, bf16[320,128]{1,0:T(8,128)(2,1)S(1)} %collective-permute-done.5.refs_2_, bf16[64,6656]{1,0:T(8,128)(2,1)S(1)} %all_gather.15.refs_3_.n0, ...), custom_call_target="tpu_custom_call" | custom-call | flops 954204160 | bytes 6291456 | tf_op jit(solution)/shard_map/pallas_call | solution.py:74
  57.7 6.2 %collective-permute-start.9 = (bf16[64,3328]{1,0:T(8,128)(2,1)S(1)}, bf16[64,3328]{1,0:T(8,128)(2,1)S(1)}, u32[]{:S(2)}, u32[]{:S(2)}) collective-permute-start(bf16[64,3328]{1,0:T(8,128)(2,1)S(1)} %get-tuple-element.14), channel_id=1, source_target_pairs={{0,4},{1,1023},{2,6},{3,1021},{4,8},{5,1},{6,10},{7,3},{8,12},{9,5... | collective-permute-start | bytes 1277960 | tf_op jit(solution)/shard_map/ppermute | solution.py:133
  63.9 1.9 %shard_map.51 = (bf16[64,3328]{1,0:T(8,128)(2,1)S(1)}, bf16[64,3328]{1,0:T(8,128)(2,1)S(1)}, bf16[64,3328]{1,0:T(8,128)(2,1)S(1)}, bf16[128,3328]{1,0:T(8,128)(2,1)S(1)}) custom-call(s32[1]{0:T(128)} %bitcast.refs_0_.core, bf16[320,128]{1,0:T(8,128)(2,1)S(1)} %bitcast.5, bf16[320,128]{1,0:T(8,128)(2,1)S(1)} %collective-permute-done.5.refs_2_, ...), custom_call_target="tpu_custom_call" | custom-call | flops 954204160 | bytes 6291456 | tf_op jit(solution)/shard_map/pallas_call | solution.py:74
  65.8 3.8 %collective-permute-start.7 = (bf16[64,3328]{1,0:T(8,128)(2,1)S(1)}, bf16[64,3328]{1,0:T(8,128)(2,1)S(1)}, u32[]{:S(2)}, u32[]{:S(2)}) collective-permute-start(bf16[64,3328]{1,0:T(8,128)(2,1)S(1)} %get-tuple-element.12), channel_id=1, source_target_pairs={{0,4},{1,1023},{2,6},{3,1021},{4,8},{5,1},{6,10},{7,3},{8,12},{9,5... | collective-permute-start | bytes 1277960 | tf_op jit(solution)/shard_map/ppermute | solution.py:133
  69.6 0.0 collective-permute-done.9
  69.6 0.1 add_convert_fusion.2
  69.7 8.6 %collective-permute-start.10 = (bf16[64,3328]{1,0:T(8,128)(2,1)S(1)}, bf16[64,3328]{1,0:T(8,128)(2,1)S(1)}, u32[]{:S(2)}, u32[]{:S(2)}) collective-permute-start(bf16[64,3328]{1,0:T(8,128)(2,1)S(1)} %add_convert_fusion.2), channel_id=1, source_target_pairs={{0,4},{1,1023},{2,6},{3,1021},{4,8},{5,1},{6,10},{7,3},{8,12},{9,5... | collective-permute-start | bytes 1277960 | tf_op jit(solution)/shard_map/ppermute | solution.py:133
  78.3 0.0 collective-permute-done.7
  78.3 0.1 add_convert_fusion.3
  78.4 5.6 %collective-permute-start.8 = (bf16[64,3328]{1,0:T(8,128)(2,1)S(1)}, bf16[64,3328]{1,0:T(8,128)(2,1)S(1)}, u32[]{:S(2)}, u32[]{:S(2)}) collective-permute-start(bf16[64,3328]{1,0:T(8,128)(2,1)S(1)} %add_convert_fusion.3), channel_id=1, source_target_pairs={{0,4},{1,1023},{2,6},{3,1021},{4,8},{5,1},{6,10},{7,3},{8,12},{9,5... | collective-permute-start | bytes 1277960 | tf_op jit(solution)/shard_map/ppermute | solution.py:133
  84.0 0.0 collective-permute-done.10
  84.0 7.0 %collective-permute-start.11 = (bf16[64,3328]{1,0:T(8,128)(2,1)S(1)}, bf16[64,3328]{1,0:T(8,128)(2,1)S(1)}, u32[]{:S(2)}, u32[]{:S(2)}) collective-permute-start(bf16[64,3328]{1,0:T(8,128)(2,1)S(1)} %collective-permute-done.10), channel_id=1, source_target_pairs={{0,1},{1,0},{2,3},{3,2},{4,5},{5,4},{6,7},{7,6},{8,9},{9,8},{10,11... | collective-permute-start | bytes 1277960 | tf_op jit(solution)/shard_map/ppermute | solution.py:133
  91.0 0.0 collective-permute-done.8
  91.0 1.4 %collective-permute-done.11 = bf16[64,3328]{1,0:T(8,128)(2,1)S(1)} collective-permute-done((bf16[64,3328]{1,0:T(8,128)(2,1)S(1)}, bf16[64,3328]{1,0:T(8,128)(2,1)S(1)}, u32[]{:S(2)}, u32[]{:S(2)}) %collective-permute-start.11) | collective-permute-done | bytes 426016 | tf_op jit(solution)/shard_map/ppermute | solution.py:133
  92.3 0.2 add_convert_fusion.1
  92.5 4.4 %collective-permute-start.12 = (bf16[64,3328]{1,0:T(8,128)(2,1)S(1)}, bf16[64,3328]{1,0:T(8,128)(2,1)S(1)}, u32[]{:S(2)}, u32[]{:S(2)}) collective-permute-start(bf16[64,3328]{1,0:T(8,128)(2,1)S(1)} %add_convert_fusion.1), channel_id=1, source_target_pairs={{0,2},{1,3},{2,0},{3,1},{4,6},{5,7},{6,4},{7,5},{8,10},{9,11},{10,... | collective-permute-start | bytes 1277960 | tf_op jit(solution)/shard_map/ppermute | solution.py:133
  96.9 1.9 %shard_map.52 = bf16[320,128]{1,0:T(8,128)(2,1)} custom-call(s32[1]{0:T(128)} %bitcast.refs_0_.core, bf16[64,6656]{1,0:T(8,128)(2,1)S(1)} %all_gather.15.refs_3_.n0, bf16[64,6656]{1,0:T(8,128)(2,1)S(1)} %all_gather.16.refs_4_.n1, bf16[64,6656]{1,0:T(8,128)(2,1)S(1)} %all_gather.17.refs_5_.f0, bf16[64,6656]{1,0:T(8,128)(2,1)S(1)} %all_gather.18.refs_6_.f1, ...), custom_call_target="tpu_custom_call" | custom-call | flops 545259520 | bytes 6291456 | tf_op jit(solution)/shard_map/pallas_call | solution.py:93
  98.8 18.8 %collective-permute-done.12 = bf16[64,3328]{1,0:T(8,128)(2,1)S(1)} collective-permute-done((bf16[64,3328]{1,0:T(8,128)(2,1)S(1)}, bf16[64,3328]{1,0:T(8,128)(2,1)S(1)}, u32[]{:S(2)}, u32[]{:S(2)}) %collective-permute-start.12) | collective-permute-done | bytes 426016 | tf_op jit(solution)/shard_map/ppermute | solution.py:133
  117.6 0.1 add_convert_fusion
  117.7 2.5 %all_gather.19 = bf16[64,6656]{1,0:T(8,128)(2,1)S(1)} all-gather(bf16[64,3328]{1,0:T(8,128)(2,1)S(1)} %add_convert_fusion), channel_id=1, replica_groups={{0,1},{2,3},{4,5},{6,7},{8,9},{10,11},{12,13},{14,15},{16,17},{18,19},{..., dimensions={1}, use_global_device_ids=true | all-gather | bytes 1277952 | tf_op jit(solution)/shard_map/all_gather | solution.py:136
  120.3 0.9 copy.6
Async XLA Ops:
  0.6 30.5 %collective-permute-start = (bf16[64,6656]{1,0:T(8,128)(2,1)}, bf16[64,6656]{1,0:T(8,128)(2,1)S(1)}, u32[]{:S(2)}, u32[]{:S(2)}) collective-permute-start(bf16[64,6656]{1,0:T(8,128)(2,1)} %w_own.1), channel_id=1, source_target_pairs={{0,4},{2,6},{4,8},{5,1},{6,10},{7,3},{8,12},{9,5},{10,14},{11,7},{... | collective-permute-start | bytes 2555912 | tf_op jit(solution)/shard_map/ppermute | solution.py:133
  1.9 34.8 %collective-permute-start.1 = (bf16[64,6656]{1,0:T(8,128)(2,1)}, bf16[64,6656]{1,0:T(8,128)(2,1)S(1)}, u32[]{:S(2)}, u32[]{:S(2)}) collective-permute-start(bf16[64,6656]{1,0:T(8,128)(2,1)} %w_own.1), channel_id=1, source_target_pairs={{1,1023},{3,1021},{60,64},{62,66},{65,61},{67,63},{124,128},{126,1... | collective-permute-start | bytes 2555912 | tf_op jit(solution)/shard_map/ppermute | solution.py:133
  26.8 29.1 %collective-permute-start.5 = (bf16[320,128]{1,0:T(8,128)(2,1)}, bf16[320,128]{1,0:T(8,128)(2,1)S(1)}, u32[]{:S(2)}, u32[]{:S(2)}) collective-permute-start(bf16[320,128]{1,0:T(8,128)(2,1)} %bitcast.3), channel_id=1, source_target_pairs={{0,1},{1,0},{2,3},{3,2},{4,5},{5,4},{6,7},{7,6},{8,9},{9,8},{10,11... | collective-permute-start | bytes 245768 | tf_op jit(solution)/shard_map/ppermute | solution.py:133
  28.7 27.2 %collective-permute-start.6 = (bf16[128,6656]{1,0:T(8,128)(2,1)}, bf16[128,6656]{1,0:T(8,128)(2,1)S(1)}, u32[]{:S(2)}, u32[]{:S(2)}) collective-permute-start(bf16[128,6656]{1,0:T(8,128)(2,1)} %refs_8_.3), channel_id=1, source_target_pairs={{0,1},{1,0},{2,3},{3,2},{4,5},{5,4},{6,7},{7,6},{8,9},{9,8},{10,11... | collective-permute-start | bytes 5111816 | tf_op jit(solution)/shard_map/ppermute | solution.py:133
  31.2 19.5 %collective-permute-start.3 = (bf16[64,6656]{1,0:T(8,128)(2,1)S(1)}, bf16[64,6656]{1,0:T(8,128)(2,1)S(1)}, u32[]{:S(2)}, u32[]{:S(2)}) collective-permute-start(bf16[64,6656]{1,0:T(8,128)(2,1)S(1)} %collective-permute-done), channel_id=1, source_target_pairs={{1,1023},{3,1021},{60,64},{62,66},{65,61},{67,63},{124,128},{126,1... | collective-permute-start | bytes 2555912 | tf_op jit(solution)/shard_map/ppermute | solution.py:133
  36.9 9.2 %collective-permute-start.2 = (bf16[32,6656]{1,0:T(8,128)(2,1)S(1)}, bf16[32,6656]{1,0:T(8,128)(2,1)S(1)}, u32[]{:S(2)}, u32[]{:S(2)}) collective-permute-start(bf16[32,6656]{1,0:T(8,128)(2,1)S(1)} %get-tuple-element.19), channel_id=1, source_target_pairs={{0,4},{2,6},{4,8},{5,1},{6,10},{7,3},{8,12},{9,5},{10,14},{11,7},{... | collective-permute-start | bytes 1277960 | tf_op jit(solution)/shard_map/ppermute | solution.py:133
  38.2 12.4 %collective-permute-start.4 = (bf16[32,6656]{1,0:T(8,128)(2,1)S(1)}, bf16[32,6656]{1,0:T(8,128)(2,1)S(1)}, u32[]{:S(2)}, u32[]{:S(2)}) collective-permute-start(bf16[32,6656]{1,0:T(8,128)(2,1)S(1)} %get-tuple-element.18), channel_id=1, source_target_pairs={{0,4},{2,6},{4,8},{5,1},{6,10},{7,3},{8,12},{9,5},{10,14},{11,7},{... | collective-permute-start | bytes 1277960 | tf_op jit(solution)/shard_map/ppermute | solution.py:133
  50.7 5.2 %copy-start.2 = (bf16[128,320]{0,1:T(8,128)(2,1)S(1)}, bf16[128,320]{0,1:T(8,128)(2,1)}, u32[]{:S(2)}) copy-start(bf16[128,320]{0,1:T(8,128)(2,1)} %param.3) | copy-start | bytes 245764
  50.8 5.1 %copy-start = (bf16[64,6656]{1,0:T(8,128)(2,1)S(1)}, bf16[64,6656]{1,0:T(8,128)(2,1)}, u32[]{:S(2)}) copy-start(bf16[64,6656]{1,0:T(8,128)(2,1)} %w_own.1) | copy-start | bytes 2555908
  50.8 5.1 %copy-start.1 = (bf16[128,6656]{1,0:T(8,128)(2,1)S(1)}, bf16[128,6656]{1,0:T(8,128)(2,1)}, u32[]{:S(2)}) copy-start(bf16[128,6656]{1,0:T(8,128)(2,1)} %refs_8_.3) | copy-start | bytes 5111812
  57.7 11.9 %collective-permute-start.9 = (bf16[64,3328]{1,0:T(8,128)(2,1)S(1)}, bf16[64,3328]{1,0:T(8,128)(2,1)S(1)}, u32[]{:S(2)}, u32[]{:S(2)}) collective-permute-start(bf16[64,3328]{1,0:T(8,128)(2,1)S(1)} %get-tuple-element.14), channel_id=1, source_target_pairs={{0,4},{1,1023},{2,6},{3,1021},{4,8},{5,1},{6,10},{7,3},{8,12},{9,5... | collective-permute-start | bytes 1277960 | tf_op jit(solution)/shard_map/ppermute | solution.py:133
  65.8 12.5 %collective-permute-start.7 = (bf16[64,3328]{1,0:T(8,128)(2,1)S(1)}, bf16[64,3328]{1,0:T(8,128)(2,1)S(1)}, u32[]{:S(2)}, u32[]{:S(2)}) collective-permute-start(bf16[64,3328]{1,0:T(8,128)(2,1)S(1)} %get-tuple-element.12), channel_id=1, source_target_pairs={{0,4},{1,1023},{2,6},{3,1021},{4,8},{5,1},{6,10},{7,3},{8,12},{9,5... | collective-permute-start | bytes 1277960 | tf_op jit(solution)/shard_map/ppermute | solution.py:133
  69.7 14.3 %collective-permute-start.10 = (bf16[64,3328]{1,0:T(8,128)(2,1)S(1)}, bf16[64,3328]{1,0:T(8,128)(2,1)S(1)}, u32[]{:S(2)}, u32[]{:S(2)}) collective-permute-start(bf16[64,3328]{1,0:T(8,128)(2,1)S(1)} %add_convert_fusion.2), channel_id=1, source_target_pairs={{0,4},{1,1023},{2,6},{3,1021},{4,8},{5,1},{6,10},{7,3},{8,12},{9,5... | collective-permute-start | bytes 1277960 | tf_op jit(solution)/shard_map/ppermute | solution.py:133
  78.4 12.5 %collective-permute-start.8 = (bf16[64,3328]{1,0:T(8,128)(2,1)S(1)}, bf16[64,3328]{1,0:T(8,128)(2,1)S(1)}, u32[]{:S(2)}, u32[]{:S(2)}) collective-permute-start(bf16[64,3328]{1,0:T(8,128)(2,1)S(1)} %add_convert_fusion.3), channel_id=1, source_target_pairs={{0,4},{1,1023},{2,6},{3,1021},{4,8},{5,1},{6,10},{7,3},{8,12},{9,5... | collective-permute-start | bytes 1277960 | tf_op jit(solution)/shard_map/ppermute | solution.py:133
  84.0 8.3 %collective-permute-start.11 = (bf16[64,3328]{1,0:T(8,128)(2,1)S(1)}, bf16[64,3328]{1,0:T(8,128)(2,1)S(1)}, u32[]{:S(2)}, u32[]{:S(2)}) collective-permute-start(bf16[64,3328]{1,0:T(8,128)(2,1)S(1)} %collective-permute-done.10), channel_id=1, source_target_pairs={{0,1},{1,0},{2,3},{3,2},{4,5},{5,4},{6,7},{7,6},{8,9},{9,8},{10,11... | collective-permute-start | bytes 1277960 | tf_op jit(solution)/shard_map/ppermute | solution.py:133
  92.5 25.1 %collective-permute-start.12 = (bf16[64,3328]{1,0:T(8,128)(2,1)S(1)}, bf16[64,3328]{1,0:T(8,128)(2,1)S(1)}, u32[]{:S(2)}, u32[]{:S(2)}) collective-permute-start(bf16[64,3328]{1,0:T(8,128)(2,1)S(1)} %add_convert_fusion.1), channel_id=1, source_target_pairs={{0,2},{1,3},{2,0},{3,1},{4,6},{5,7},{6,4},{7,5},{8,10},{9,11},{10,... | collective-permute-start | bytes 1277960 | tf_op jit(solution)/shard_map/ppermute | solution.py:133

commit v4 on v3

--- a/solution.py
+++ b/solution.py
@@ -122,7 +122,7 @@
     inner = [pair for pair in ring if not crosses(pair)]
     outer = [pair for pair in ring if crosses(pair)]
     swap_core = pairs_of(lambda p, r: (p, r ^ 1))
-    swap_far = pairs_of(lambda p, r: (p, r ^ 2))
+    far_groups = [[g, g + 2] for g in range(2)]
     core_groups = [[g, g + 1] for g in range(0, n_r, 2)]
 
     def on_device(tokens, weight, cotangent):
@@ -157,8 +157,9 @@
         g_2 = send(b16(f32(g_2) + f32(one_2)), ring)
         got = send(g_1, swap_core)
         mine = b16(f32(own) + f32(g_2) + f32(got))
-        other = send(mine, swap_far)
-        weight_grad = gather(b16(f32(mine) + f32(other)), 1)
+        both = lax.all_gather(mine, "rep", axis=0, tiled=True, axis_index_groups=far_groups)
+        rows = weight.shape[0]
+        weight_grad = gather(b16(f32(both[:rows]) + f32(both[rows:])), 1)
         token_grad = token_gradient(which, pairs, weight, slope_1, slope_2, tokens.shape[1]).T
         return (token_grad, weight_grad)
 

time: 122 us -> 121 us (level)
  blocking collectives: 12.4 us -> 36.4 us
  waiting for transfers between devices: 26.5 us -> 6.35 us
  starting transfers between devices: 74.1 us -> 69.7 us
    all_gather x0 -> x1, blocking collectives: none -> 23.9 us  [on_device(): lax.all_gather(mine, 'rep', axis=0, tiled=True, axis_index_groups=far_gro...]
    ppermute x13 -> x12, waiting for transfers between devices: 26.5 us -> 6.35 us  [send(): return lax.ppermute(v, AXES, how)]
    ppermute x13 -> x12, starting transfers between devices: 74.1 us -> 69.7 us  [send(): return lax.ppermute(v, AXES, how)]
  transfers between devices with their start and end apart: 13 -> 12, of which waited for: 4 -> 2; matrix products, arithmetic and copies ran while one was open for 0% -> 0% of each run, Pallas kernels for 3% -> 3%
where the time goes in v4:
time: 121 us; the launch traced here: 120 us
  starting transfers between devices  69.7 us (58%)
  blocking collectives  36.4 us (30%)
  waiting for transfers between devices  6.35 us (5%)
  Pallas kernels  5.54 us (5%)
    ppermute x12, starting transfers between devices, send(): return lax.ppermute(v, AXES, how)  69.7 us
    all_gather x1, blocking collectives, on_device(): lax.all_gather(mine, 'rep', axis=0, tiled=True, axis_index_groups=far_gro...  23.9 us
    all_gather x5, blocking collectives, gather(): lax.all_gather(v, 'rep', axis=axis, tiled=True, axis_index_groups=core_gr...  12.4 us
    ppermute x12, waiting for transfers between devices, send(): return lax.ppermute(v, AXES, how)  6.35 us
    pallas_call x2, Pallas kernels, slopes(): pl.pallas_call(lambda *refs: slope_kernel(own_cols, *refs), grid_spec=plt...  3.63 us
  transfers between devices with their start and end apart: 12, of which 2 were waited for; matrix products, arithmetic and copies ran while one was open for 0% of the time, Pallas kernels for 3%

profile of v4, /device:TPU:1, one launch (start us, length us, event | category | flops | bytes accessed | tf_op | source)
XLA Modules:
  0.0 120.5 jit_solution(12604841855333899169)
XLA Ops:
  0.6 1.3 %collective-permute-start = (bf16[64,6656]{1,0:T(8,128)(2,1)}, bf16[64,6656]{1,0:T(8,128)(2,1)S(1)}, u32[]{:S(2)}, u32[]{:S(2)}) collective-permute-start(bf16[64,6656]{1,0:T(8,128)(2,1)} %w_own.1), channel_id=1, source_target_pairs={{0,4},{2,6},{4,8},{5,1},{6,10},{7,3},{8,12},{9,5},{10,14},{11,7},{... | collective-permute-start | bytes 2555912 | tf_op jit(solution)/shard_map/ppermute | solution.py:133
  1.9 24.9 %collective-permute-start.1 = (bf16[64,6656]{1,0:T(8,128)(2,1)}, bf16[64,6656]{1,0:T(8,128)(2,1)S(1)}, u32[]{:S(2)}, u32[]{:S(2)}) collective-permute-start(bf16[64,6656]{1,0:T(8,128)(2,1)} %w_own.1), channel_id=1, source_target_pairs={{1,1023},{3,1021},{60,64},{62,66},{65,61},{67,63},{124,128},{126,1... | collective-permute-start | bytes 2555912 | tf_op jit(solution)/shard_map/ppermute | solution.py:133
  26.8 1.9 %collective-permute-start.5 = (bf16[320,128]{1,0:T(8,128)(2,1)}, bf16[320,128]{1,0:T(8,128)(2,1)S(1)}, u32[]{:S(2)}, u32[]{:S(2)}) collective-permute-start(bf16[320,128]{1,0:T(8,128)(2,1)} %bitcast.3), channel_id=1, source_target_pairs={{0,1},{1,0},{2,3},{3,2},{4,5},{5,4},{6,7},{7,6},{8,9},{9,8},{10,11... | collective-permute-start | bytes 245768 | tf_op jit(solution)/shard_map/ppermute | solution.py:133
  28.7 2.4 %collective-permute-start.6 = (bf16[128,6656]{1,0:T(8,128)(2,1)}, bf16[128,6656]{1,0:T(8,128)(2,1)S(1)}, u32[]{:S(2)}, u32[]{:S(2)}) collective-permute-start(bf16[128,6656]{1,0:T(8,128)(2,1)} %refs_8_.3), channel_id=1, source_target_pairs={{0,1},{1,0},{2,3},{3,2},{4,5},{5,4},{6,7},{7,6},{8,9},{9,8},{10,11... | collective-permute-start | bytes 5111816 | tf_op jit(solution)/shard_map/ppermute | solution.py:133
  31.2 0.0 collective-permute-done
  31.2 5.5 %collective-permute-start.3 = (bf16[64,6656]{1,0:T(8,128)(2,1)S(1)}, bf16[64,6656]{1,0:T(8,128)(2,1)S(1)}, u32[]{:S(2)}, u32[]{:S(2)}) collective-permute-start(bf16[64,6656]{1,0:T(8,128)(2,1)S(1)} %collective-permute-done), channel_id=1, source_target_pairs={{1,1023},{3,1021},{60,64},{62,66},{65,61},{67,63},{124,128},{126,1... | collective-permute-start | bytes 2555912 | tf_op jit(solution)/shard_map/ppermute | solution.py:133
  36.7 0.0 collective-permute-done.1
  36.7 0.2 add.29
  36.9 0.1 fusion
  36.9 1.3 %collective-permute-start.2 = (bf16[32,6656]{1,0:T(8,128)(2,1)S(1)}, bf16[32,6656]{1,0:T(8,128)(2,1)S(1)}, u32[]{:S(2)}, u32[]{:S(2)}) collective-permute-start(bf16[32,6656]{1,0:T(8,128)(2,1)S(1)} %get-tuple-element.19), channel_id=1, source_target_pairs={{0,4},{2,6},{4,8},{5,1},{6,10},{7,3},{8,12},{9,5},{10,14},{11,7},{... | collective-permute-start | bytes 1277960 | tf_op jit(solution)/shard_map/ppermute | solution.py:133
  38.2 1.3 %collective-permute-start.4 = (bf16[32,6656]{1,0:T(8,128)(2,1)S(1)}, bf16[32,6656]{1,0:T(8,128)(2,1)S(1)}, u32[]{:S(2)}, u32[]{:S(2)}) collective-permute-start(bf16[32,6656]{1,0:T(8,128)(2,1)S(1)} %get-tuple-element.18), channel_id=1, source_target_pairs={{0,4},{2,6},{4,8},{5,1},{6,10},{7,3},{8,12},{9,5},{10,14},{11,7},{... | collective-permute-start | bytes 1277960 | tf_op jit(solution)/shard_map/ppermute | solution.py:133
  39.5 2.4 %all_gather.18.refs_3_.n0 = bf16[64,6656]{1,0:T(8,128)(2,1)S(1)} all-gather(bf16[32,6656]{1,0:T(8,128)(2,1)S(1)} %get-tuple-element.19), channel_id=1, replica_groups={{0,1},{2,3},{4,5},{6,7},{8,9},{10,11},{12,13},{14,15},{16,17},{18,19},{..., dimensions={0}, use_global_device_ids=true | all-gather | bytes 1277952 | tf_op jit(solution)/shard_map/all_gather | solution.py:136
  42.0 2.4 %all_gather.19.refs_4_.n1 = bf16[64,6656]{1,0:T(8,128)(2,1)S(1)} all-gather(bf16[32,6656]{1,0:T(8,128)(2,1)S(1)} %get-tuple-element.18), channel_id=1, replica_groups={{0,1},{2,3},{4,5},{6,7},{8,9},{10,11},{12,13},{14,15},{16,17},{18,19},{..., dimensions={0}, use_global_device_ids=true | all-gather | bytes 1277952 | tf_op jit(solution)/shard_map/all_gather | solution.py:136
  44.4 1.7 %collective-permute-done.2 = bf16[32,6656]{1,0:T(8,128)(2,1)S(1)} collective-permute-done((bf16[32,6656]{1,0:T(8,128)(2,1)S(1)}, bf16[32,6656]{1,0:T(8,128)(2,1)S(1)}, u32[]{:S(2)}, u32[]{:S(2)}) %collective-permute-start.2) | collective-permute-done | bytes 426016 | tf_op jit(solution)/shard_map/ppermute | solution.py:133
  46.1 4.6 %collective-permute-done.4 = bf16[32,6656]{1,0:T(8,128)(2,1)S(1)} collective-permute-done((bf16[32,6656]{1,0:T(8,128)(2,1)S(1)}, bf16[32,6656]{1,0:T(8,128)(2,1)S(1)}, u32[]{:S(2)}, u32[]{:S(2)}) %collective-permute-start.4) | collective-permute-done | bytes 426016 | tf_op jit(solution)/shard_map/ppermute | solution.py:133
  50.7 0.0 collective-permute-done.3
  50.7 0.0 copy-start.2
  50.7 0.1 slice_add_fusion
  50.8 0.0 copy-start
  50.8 0.0 copy-start.1
  50.8 2.7 %all_gather.20.refs_5_.f0 = bf16[64,6656]{1,0:T(8,128)(2,1)S(1)} all-gather(bf16[32,6656]{1,0:T(8,128)(2,1)S(1)} %get-tuple-element.17), channel_id=1, replica_groups={{0,1},{2,3},{4,5},{6,7},{8,9},{10,11},{12,13},{14,15},{16,17},{18,19},{..., dimensions={0}, use_global_device_ids=true | all-gather | bytes 1277952 | tf_op jit(solution)/shard_map/all_gather | solution.py:136
  53.5 2.4 %all_gather.21.refs_6_.f1 = bf16[64,6656]{1,0:T(8,128)(2,1)S(1)} all-gather(bf16[32,6656]{1,0:T(8,128)(2,1)S(1)} %get-tuple-element.16), channel_id=1, replica_groups={{0,1},{2,3},{4,5},{6,7},{8,9},{10,11},{12,13},{14,15},{16,17},{18,19},{..., dimensions={0}, use_global_device_ids=true | all-gather | bytes 1277952 | tf_op jit(solution)/shard_map/all_gather | solution.py:136
  55.9 0.0 collective-permute-done.5.refs_2_
  55.9 0.0 collective-permute-done.6.refs_9_
  55.9 0.0 copy-done.2
  55.9 0.0 copy-done
  55.9 0.0 copy-done.1
  55.9 1.8 %shard_map.50 = (bf16[64,3328]{1,0:T(8,128)(2,1)S(1)}, bf16[64,3328]{1,0:T(8,128)(2,1)S(1)}, bf16[128,3328]{1,0:T(8,128)(2,1)S(1)}) custom-call(s32[1]{0:T(128)} %bitcast.refs_0_.core, bf16[320,128]{1,0:T(8,128)(2,1)S(1)} %bitcast.4, bf16[320,128]{1,0:T(8,128)(2,1)S(1)} %collective-permute-done.5.refs_2_, bf16[64,6656]{1,0:T(8,128)(2,1)S(1)} %all_gather.18.refs_3_.n0, ...), custom_call_target="tpu_custom_call" | custom-call | flops 954204160 | bytes 6291456 | tf_op jit(solution)/shard_map/pallas_call | solution.py:74
  57.7 6.2 %collective-permute-start.9 = (bf16[64,3328]{1,0:T(8,128)(2,1)S(1)}, bf16[64,3328]{1,0:T(8,128)(2,1)S(1)}, u32[]{:S(2)}, u32[]{:S(2)}) collective-permute-start(bf16[64,3328]{1,0:T(8,128)(2,1)S(1)} %get-tuple-element.14), channel_id=1, source_target_pairs={{0,4},{1,1023},{2,6},{3,1021},{4,8},{5,1},{6,10},{7,3},{8,12},{9,5... | collective-permute-start | bytes 1277960 | tf_op jit(solution)/shard_map/ppermute | solution.py:133
  63.9 1.9 %shard_map.51 = (bf16[64,3328]{1,0:T(8,128)(2,1)S(1)}, bf16[64,3328]{1,0:T(8,128)(2,1)S(1)}, bf16[64,3328]{1,0:T(8,128)(2,1)S(1)}, bf16[128,3328]{1,0:T(8,128)(2,1)S(1)}) custom-call(s32[1]{0:T(128)} %bitcast.refs_0_.core, bf16[320,128]{1,0:T(8,128)(2,1)S(1)} %bitcast.5, bf16[320,128]{1,0:T(8,128)(2,1)S(1)} %collective-permute-done.5.refs_2_, ...), custom_call_target="tpu_custom_call" | custom-call | flops 954204160 | bytes 6291456 | tf_op jit(solution)/shard_map/pallas_call | solution.py:74
  65.8 3.8 %collective-permute-start.7 = (bf16[64,3328]{1,0:T(8,128)(2,1)S(1)}, bf16[64,3328]{1,0:T(8,128)(2,1)S(1)}, u32[]{:S(2)}, u32[]{:S(2)}) collective-permute-start(bf16[64,3328]{1,0:T(8,128)(2,1)S(1)} %get-tuple-element.12), channel_id=1, source_target_pairs={{0,4},{1,1023},{2,6},{3,1021},{4,8},{5,1},{6,10},{7,3},{8,12},{9,5... | collective-permute-start | bytes 1277960 | tf_op jit(solution)/shard_map/ppermute | solution.py:133
  69.6 0.0 collective-permute-done.9
  69.6 0.1 add_convert_fusion.2
  69.7 8.6 %collective-permute-start.10 = (bf16[64,3328]{1,0:T(8,128)(2,1)S(1)}, bf16[64,3328]{1,0:T(8,128)(2,1)S(1)}, u32[]{:S(2)}, u32[]{:S(2)}) collective-permute-start(bf16[64,3328]{1,0:T(8,128)(2,1)S(1)} %add_convert_fusion.2), channel_id=1, source_target_pairs={{0,4},{1,1023},{2,6},{3,1021},{4,8},{5,1},{6,10},{7,3},{8,12},{9,5... | collective-permute-start | bytes 1277960 | tf_op jit(solution)/shard_map/ppermute | solution.py:133
  78.3 0.0 collective-permute-done.7
  78.3 0.1 add_convert_fusion.3
  78.4 5.6 %collective-permute-start.8 = (bf16[64,3328]{1,0:T(8,128)(2,1)S(1)}, bf16[64,3328]{1,0:T(8,128)(2,1)S(1)}, u32[]{:S(2)}, u32[]{:S(2)}) collective-permute-start(bf16[64,3328]{1,0:T(8,128)(2,1)S(1)} %add_convert_fusion.3), channel_id=1, source_target_pairs={{0,4},{1,1023},{2,6},{3,1021},{4,8},{5,1},{6,10},{7,3},{8,12},{9,5... | collective-permute-start | bytes 1277960 | tf_op jit(solution)/shard_map/ppermute | solution.py:133
  84.0 0.0 collective-permute-done.10
  84.0 7.0 %collective-permute-start.11 = (bf16[64,3328]{1,0:T(8,128)(2,1)S(1)}, bf16[64,3328]{1,0:T(8,128)(2,1)S(1)}, u32[]{:S(2)}, u32[]{:S(2)}) collective-permute-start(bf16[64,3328]{1,0:T(8,128)(2,1)S(1)} %collective-permute-done.10), channel_id=1, source_target_pairs={{0,1},{1,0},{2,3},{3,2},{4,5},{5,4},{6,7},{7,6},{8,9},{9,8},{10,11... | collective-permute-start | bytes 1277960 | tf_op jit(solution)/shard_map/ppermute | solution.py:133
  91.0 1.9 %shard_map.52 = bf16[320,128]{1,0:T(8,128)(2,1)} custom-call(s32[1]{0:T(128)} %bitcast.refs_0_.core, bf16[64,6656]{1,0:T(8,128)(2,1)S(1)} %all_gather.18.refs_3_.n0, bf16[64,6656]{1,0:T(8,128)(2,1)S(1)} %all_gather.19.refs_4_.n1, bf16[64,6656]{1,0:T(8,128)(2,1)S(1)} %all_gather.20.refs_5_.f0, bf16[64,6656]{1,0:T(8,128)(2,1)S(1)} %all_gather.21.refs_6_.f1, ...), custom_call_target="tpu_custom_call" | custom-call | flops 545259520 | bytes 6291456 | tf_op jit(solution)/shard_map/pallas_call | solution.py:93
  92.9 0.0 collective-permute-done.8
  92.9 0.0 collective-permute-done.11
  92.9 0.2 add_convert_fusion.1
  93.0 23.9 %all_gather.22 = bf16[128,3328]{1,0:T(8,128)(2,1)S(1)} all-gather(bf16[64,3328]{1,0:T(8,128)(2,1)S(1)} %add_convert_fusion.1), channel_id=1, replica_groups={{0,2},{1,3},{4,6},{5,7},{8,10},{9,11},{12,14},{13,15},{16,18},{17,19},{..., dimensions={0}, use_global_device_ids=true | all-gather | bytes 1277952 | tf_op jit(solution)/shard_map/all_gather | solution.py:160
  117.0 0.1 add_convert_fusion
  117.1 2.5 %all_gather.23 = bf16[64,6656]{1,0:T(8,128)(2,1)S(1)} all-gather(bf16[64,3328]{1,0:T(8,128)(2,1)S(1)} %add_convert_fusion), channel_id=1, replica_groups={{0,1},{2,3},{4,5},{6,7},{8,9},{10,11},{12,13},{14,15},{16,17},{18,19},{..., dimensions={1}, use_global_device_ids=true | all-gather | bytes 1277952 | tf_op jit(solution)/shard_map/all_gather | solution.py:136
  119.6 0.9 copy.6
Async XLA Ops:
  0.6 30.5 %collective-permute-start = (bf16[64,6656]{1,0:T(8,128)(2,1)}, bf16[64,6656]{1,0:T(8,128)(2,1)S(1)}, u32[]{:S(2)}, u32[]{:S(2)}) collective-permute-start(bf16[64,6656]{1,0:T(8,128)(2,1)} %w_own.1), channel_id=1, source_target_pairs={{0,4},{2,6},{4,8},{5,1},{6,10},{7,3},{8,12},{9,5},{10,14},{11,7},{... | collective-permute-start | bytes 2555912 | tf_op jit(solution)/shard_map/ppermute | solution.py:133
  1.9 34.8 %collective-permute-start.1 = (bf16[64,6656]{1,0:T(8,128)(2,1)}, bf16[64,6656]{1,0:T(8,128)(2,1)S(1)}, u32[]{:S(2)}, u32[]{:S(2)}) collective-permute-start(bf16[64,6656]{1,0:T(8,128)(2,1)} %w_own.1), channel_id=1, source_target_pairs={{1,1023},{3,1021},{60,64},{62,66},{65,61},{67,63},{124,128},{126,1... | collective-permute-start | bytes 2555912 | tf_op jit(solution)/shard_map/ppermute | solution.py:133
  26.8 29.1 %collective-permute-start.5 = (bf16[320,128]{1,0:T(8,128)(2,1)}, bf16[320,128]{1,0:T(8,128)(2,1)S(1)}, u32[]{:S(2)}, u32[]{:S(2)}) collective-permute-start(bf16[320,128]{1,0:T(8,128)(2,1)} %bitcast.3), channel_id=1, source_target_pairs={{0,1},{1,0},{2,3},{3,2},{4,5},{5,4},{6,7},{7,6},{8,9},{9,8},{10,11... | collective-permute-start | bytes 245768 | tf_op jit(solution)/shard_map/ppermute | solution.py:133
  28.7 27.2 %collective-permute-start.6 = (bf16[128,6656]{1,0:T(8,128)(2,1)}, bf16[128,6656]{1,0:T(8,128)(2,1)S(1)}, u32[]{:S(2)}, u32[]{:S(2)}) collective-permute-start(bf16[128,6656]{1,0:T(8,128)(2,1)} %refs_8_.3), channel_id=1, source_target_pairs={{0,1},{1,0},{2,3},{3,2},{4,5},{5,4},{6,7},{7,6},{8,9},{9,8},{10,11... | collective-permute-start | bytes 5111816 | tf_op jit(solution)/shard_map/ppermute | solution.py:133
  31.2 19.5 %collective-permute-start.3 = (bf16[64,6656]{1,0:T(8,128)(2,1)S(1)}, bf16[64,6656]{1,0:T(8,128)(2,1)S(1)}, u32[]{:S(2)}, u32[]{:S(2)}) collective-permute-start(bf16[64,6656]{1,0:T(8,128)(2,1)S(1)} %collective-permute-done), channel_id=1, source_target_pairs={{1,1023},{3,1021},{60,64},{62,66},{65,61},{67,63},{124,128},{126,1... | collective-permute-start | bytes 2555912 | tf_op jit(solution)/shard_map/ppermute | solution.py:133
  36.9 9.2 %collective-permute-start.2 = (bf16[32,6656]{1,0:T(8,128)(2,1)S(1)}, bf16[32,6656]{1,0:T(8,128)(2,1)S(1)}, u32[]{:S(2)}, u32[]{:S(2)}) collective-permute-start(bf16[32,6656]{1,0:T(8,128)(2,1)S(1)} %get-tuple-element.19), channel_id=1, source_target_pairs={{0,4},{2,6},{4,8},{5,1},{6,10},{7,3},{8,12},{9,5},{10,14},{11,7},{... | collective-permute-start | bytes 1277960 | tf_op jit(solution)/shard_map/ppermute | solution.py:133
  38.2 12.4 %collective-permute-start.4 = (bf16[32,6656]{1,0:T(8,128)(2,1)S(1)}, bf16[32,6656]{1,0:T(8,128)(2,1)S(1)}, u32[]{:S(2)}, u32[]{:S(2)}) collective-permute-start(bf16[32,6656]{1,0:T(8,128)(2,1)S(1)} %get-tuple-element.18), channel_id=1, source_target_pairs={{0,4},{2,6},{4,8},{5,1},{6,10},{7,3},{8,12},{9,5},{10,14},{11,7},{... | collective-permute-start | bytes 1277960 | tf_op jit(solution)/shard_map/ppermute | solution.py:133
  50.7 5.2 %copy-start.2 = (bf16[128,320]{0,1:T(8,128)(2,1)S(1)}, bf16[128,320]{0,1:T(8,128)(2,1)}, u32[]{:S(2)}) copy-start(bf16[128,320]{0,1:T(8,128)(2,1)} %param.3) | copy-start | bytes 245764
  50.8 5.1 %copy-start = (bf16[64,6656]{1,0:T(8,128)(2,1)S(1)}, bf16[64,6656]{1,0:T(8,128)(2,1)}, u32[]{:S(2)}) copy-start(bf16[64,6656]{1,0:T(8,128)(2,1)} %w_own.1) | copy-start | bytes 2555908
  50.8 5.1 %copy-start.1 = (bf16[128,6656]{1,0:T(8,128)(2,1)S(1)}, bf16[128,6656]{1,0:T(8,128)(2,1)}, u32[]{:S(2)}) copy-start(bf16[128,6656]{1,0:T(8,128)(2,1)} %refs_8_.3) | copy-start | bytes 5111812
  57.7 11.9 %collective-permute-start.9 = (bf16[64,3328]{1,0:T(8,128)(2,1)S(1)}, bf16[64,3328]{1,0:T(8,128)(2,1)S(1)}, u32[]{:S(2)}, u32[]{:S(2)}) collective-permute-start(bf16[64,3328]{1,0:T(8,128)(2,1)S(1)} %get-tuple-element.14), channel_id=1, source_target_pairs={{0,4},{1,1023},{2,6},{3,1021},{4,8},{5,1},{6,10},{7,3},{8,12},{9,5... | collective-permute-start | bytes 1277960 | tf_op jit(solution)/shard_map/ppermute | solution.py:133
  65.8 12.5 %collective-permute-start.7 = (bf16[64,3328]{1,0:T(8,128)(2,1)S(1)}, bf16[64,3328]{1,0:T(8,128)(2,1)S(1)}, u32[]{:S(2)}, u32[]{:S(2)}) collective-permute-start(bf16[64,3328]{1,0:T(8,128)(2,1)S(1)} %get-tuple-element.12), channel_id=1, source_target_pairs={{0,4},{1,1023},{2,6},{3,1021},{4,8},{5,1},{6,10},{7,3},{8,12},{9,5... | collective-permute-start | bytes 1277960 | tf_op jit(solution)/shard_map/ppermute | solution.py:133
  69.7 14.3 %collective-permute-start.10 = (bf16[64,3328]{1,0:T(8,128)(2,1)S(1)}, bf16[64,3328]{1,0:T(8,128)(2,1)S(1)}, u32[]{:S(2)}, u32[]{:S(2)}) collective-permute-start(bf16[64,3328]{1,0:T(8,128)(2,1)S(1)} %add_convert_fusion.2), channel_id=1, source_target_pairs={{0,4},{1,1023},{2,6},{3,1021},{4,8},{5,1},{6,10},{7,3},{8,12},{9,5... | collective-permute-start | bytes 1277960 | tf_op jit(solution)/shard_map/ppermute | solution.py:133
  78.4 14.5 %collective-permute-start.8 = (bf16[64,3328]{1,0:T(8,128)(2,1)S(1)}, bf16[64,3328]{1,0:T(8,128)(2,1)S(1)}, u32[]{:S(2)}, u32[]{:S(2)}) collective-permute-start(bf16[64,3328]{1,0:T(8,128)(2,1)S(1)} %add_convert_fusion.3), channel_id=1, source_target_pairs={{0,4},{1,1023},{2,6},{3,1021},{4,8},{5,1},{6,10},{7,3},{8,12},{9,5... | collective-permute-start | bytes 1277960 | tf_op jit(solution)/shard_map/ppermute | solution.py:133
  84.0 8.9 %collective-permute-start.11 = (bf16[64,3328]{1,0:T(8,128)(2,1)S(1)}, bf16[64,3328]{1,0:T(8,128)(2,1)S(1)}, u32[]{:S(2)}, u32[]{:S(2)}) collective-permute-start(bf16[64,3328]{1,0:T(8,128)(2,1)S(1)} %collective-permute-done.10), channel_id=1, source_target_pairs={{0,1},{1,0},{2,3},{3,2},{4,5},{5,4},{6,7},{7,6},{8,9},{9,8},{10,11... | collective-permute-start | bytes 1277960 | tf_op jit(solution)/shard_map/ppermute | solution.py:133

commit v5 on v4

--- a/solution.py
+++ b/solution.py
@@ -139,11 +139,11 @@
         b16 = lambda v: v.astype(jnp.bfloat16)
         step_in = send(weight, inner)
         step_out = send(weight, outer)
-        far_out = send(step_in, outer)
-        step = step_in + step_out
-        near = [step[:half], step[half:]]
+        parts = lax.optimization_barrier((step_in[:half], step_in[half:]))
+        far_out = [send(v, outer) for v in parts]
+        near = [parts[0] + step_out[:half], parts[1] + step_out[half:]]
         far = [send(v, inner) for v in near]
-        far = [far[0] + far_out[:half], far[1] + far_out[half:]]
+        far = [v + w for v, w in zip(far, far_out)]
         cot_b = send(cotangent, swap_core)
         tok_a = tokens.T
         tok_b = send(tok_a, swap_core)

time: 121 us -> 122 us (level)
  starting transfers between devices: 69.7 us -> 72.8 us
  waiting for transfers between devices: 6.35 us -> 3.98 us
    ppermute x12 -> x13, starting transfers between devices: 69.7 us -> 72.8 us  [send(): return lax.ppermute(v, AXES, how)]
    ppermute x12 -> x13, waiting for transfers between devices: 6.35 us -> 3.98 us  [send(): return lax.ppermute(v, AXES, how)]
  transfers between devices with their start and end apart: 12 -> 13, of which waited for: 2 -> 2; matrix products, arithmetic and copies ran while one was open for 0% -> 0% of each run, Pallas kernels for 3% -> 3%
where the time goes in v5:
time: 122 us
  starting transfers between devices  72.8 us (60%)
  blocking collectives  36.8 us (30%)
  Pallas kernels  5.54 us (5%)
  waiting for transfers between devices  3.98 us (3%)
    ppermute x13, starting transfers between devices, send(): return lax.ppermute(v, AXES, how)  72.8 us
    all_gather x1, blocking collectives, on_device(): lax.all_gather(mine, 'rep', axis=0, tiled=True, axis_index_groups=far_gro...  24.6 us
    all_gather x5, blocking collectives, gather(): lax.all_gather(v, 'rep', axis=axis, tiled=True, axis_index_groups=core_gr...  12.2 us
    ppermute x13, waiting for transfers between devices, send(): return lax.ppermute(v, AXES, how)  3.98 us
    pallas_call x2, Pallas kernels, slopes(): pl.pallas_call(lambda *refs: slope_kernel(own_cols, *refs), grid_spec=plt...  3.63 us
  transfers between devices with their start and end apart: 13, of which 2 were waited for; matrix products, arithmetic and copies ran while one was open for 0% of the time, Pallas kernels for 3%

profile of v5, /device:TPU:1, one launch (start us, length us, event | category | flops | bytes accessed | tf_op | source)
XLA Modules:
  0.0 121.7 jit_solution(7728973772149841505)
XLA Ops:
  0.6 1.3 %collective-permute-start = (bf16[64,6656]{1,0:T(8,128)(2,1)}, bf16[64,6656]{1,0:T(8,128)(2,1)S(1)}, u32[]{:S(2)}, u32[]{:S(2)}) collective-permute-start(bf16[64,6656]{1,0:T(8,128)(2,1)} %w_own.1), channel_id=1, source_target_pairs={{0,4},{2,6},{4,8},{5,1},{6,10},{7,3},{8,12},{9,5},{10,14},{11,7},{... | collective-permute-start | bytes 2555912 | tf_op jit(solution)/shard_map/ppermute | solution.py:133
  1.9 24.9 %collective-permute-start.1 = (bf16[64,6656]{1,0:T(8,128)(2,1)}, bf16[64,6656]{1,0:T(8,128)(2,1)S(1)}, u32[]{:S(2)}, u32[]{:S(2)}) collective-permute-start(bf16[64,6656]{1,0:T(8,128)(2,1)} %w_own.1), channel_id=1, source_target_pairs={{1,1023},{3,1021},{60,64},{62,66},{65,61},{67,63},{124,128},{126,1... | collective-permute-start | bytes 2555912 | tf_op jit(solution)/shard_map/ppermute | solution.py:133
  26.8 1.9 %collective-permute-start.7 = (bf16[128,6656]{1,0:T(8,128)(2,1)}, bf16[128,6656]{1,0:T(8,128)(2,1)S(1)}, u32[]{:S(2)}, u32[]{:S(2)}) collective-permute-start(bf16[128,6656]{1,0:T(8,128)(2,1)} %refs_8_.3), channel_id=1, source_target_pairs={{0,1},{1,0},{2,3},{3,2},{4,5},{5,4},{6,7},{7,6},{8,9},{9,8},{10,11... | collective-permute-start | bytes 5111816 | tf_op jit(solution)/shard_map/ppermute | solution.py:133
  28.7 0.0 collective-permute-done
  28.8 0.1 fusion
  28.8 7.9 %collective-permute-start.5 = (bf16[32,6656]{1,0:T(8,128)(2,1)S(1)}, bf16[32,6656]{1,0:T(8,128)(2,1)S(1)}, u32[]{:S(2)}, u32[]{:S(2)}) collective-permute-start(bf16[32,6656]{1,0:T(8,128)(2,1)S(1)} %get-tuple-element.12), channel_id=1, source_target_pairs={{1,1023},{3,1021},{60,64},{62,66},{65,61},{67,63},{124,128},{126,1... | collective-permute-start | bytes 1277960 | tf_op jit(solution)/shard_map/ppermute | solution.py:133
  36.7 1.3 %collective-permute-start.3 = (bf16[32,6656]{1,0:T(8,128)(2,1)S(1)}, bf16[32,6656]{1,0:T(8,128)(2,1)S(1)}, u32[]{:S(2)}, u32[]{:S(2)}) collective-permute-start(bf16[32,6656]{1,0:T(8,128)(2,1)S(1)} %get-tuple-element.11), channel_id=1, source_target_pairs={{1,1023},{3,1021},{60,64},{62,66},{65,61},{67,63},{124,128},{126,1... | collective-permute-start | bytes 1277960 | tf_op jit(solution)/shard_map/ppermute | solution.py:133
  38.0 0.0 collective-permute-done.1
  38.0 0.1 slice_add_fusion
  38.2 0.0 copy-start.2
  38.2 1.4 %collective-permute-start.4 = (bf16[32,6656]{1,0:T(8,128)(2,1)S(1)}, bf16[32,6656]{1,0:T(8,128)(2,1)S(1)}, u32[]{:S(2)}, u32[]{:S(2)}) collective-permute-start(bf16[32,6656]{1,0:T(8,128)(2,1)S(1)} %get-tuple-element.20), channel_id=1, source_target_pairs={{0,4},{2,6},{4,8},{5,1},{6,10},{7,3},{8,12},{9,5},{10,14},{11,7},{... | collective-permute-start | bytes 1277960 | tf_op jit(solution)/shard_map/ppermute | solution.py:133
  39.6 1.3 %collective-permute-start.2 = (bf16[32,6656]{1,0:T(8,128)(2,1)S(1)}, bf16[32,6656]{1,0:T(8,128)(2,1)S(1)}, u32[]{:S(2)}, u32[]{:S(2)}) collective-permute-start(bf16[32,6656]{1,0:T(8,128)(2,1)S(1)} %get-tuple-element.21), channel_id=1, source_target_pairs={{0,4},{2,6},{4,8},{5,1},{6,10},{7,3},{8,12},{9,5},{10,14},{11,7},{... | collective-permute-start | bytes 1277960 | tf_op jit(solution)/shard_map/ppermute | solution.py:133
  40.9 2.4 %all_gather.18.refs_3_.n0 = bf16[64,6656]{1,0:T(8,128)(2,1)S(1)} all-gather(bf16[32,6656]{1,0:T(8,128)(2,1)S(1)} %get-tuple-element.21), channel_id=1, replica_groups={{0,1},{2,3},{4,5},{6,7},{8,9},{10,11},{12,13},{14,15},{16,17},{18,19},{..., dimensions={0}, use_global_device_ids=true | all-gather | bytes 1277952 | tf_op jit(solution)/shard_map/all_gather | solution.py:136
  43.3 2.4 %all_gather.19.refs_4_.n1 = bf16[64,6656]{1,0:T(8,128)(2,1)S(1)} all-gather(bf16[32,6656]{1,0:T(8,128)(2,1)S(1)} %get-tuple-element.20), channel_id=1, replica_groups={{0,1},{2,3},{4,5},{6,7},{8,9},{10,11},{12,13},{14,15},{16,17},{18,19},{..., dimensions={0}, use_global_device_ids=true | all-gather | bytes 1277952 | tf_op jit(solution)/shard_map/all_gather | solution.py:136
  45.7 1.7 %collective-permute-done.4 = bf16[32,6656]{1,0:T(8,128)(2,1)S(1)} collective-permute-done((bf16[32,6656]{1,0:T(8,128)(2,1)S(1)}, bf16[32,6656]{1,0:T(8,128)(2,1)S(1)}, u32[]{:S(2)}, u32[]{:S(2)}) %collective-permute-start.4) | collective-permute-done | bytes 426016 | tf_op jit(solution)/shard_map/ppermute | solution.py:133
  47.5 0.0 copy-done.2
  47.5 1.9 %collective-permute-start.6 = (bf16[320,128]{1,0:T(8,128)(2,1)S(1)}, bf16[320,128]{1,0:T(8,128)(2,1)S(1)}, u32[]{:S(2)}, u32[]{:S(2)}) collective-permute-start(bf16[320,128]{1,0:T(8,128)(2,1)S(1)} %bitcast.3), channel_id=1, source_target_pairs={{0,1},{1,0},{2,3},{3,2},{4,5},{5,4},{6,7},{7,6},{8,9},{9,8},{10,11... | collective-permute-start | bytes 245768 | tf_op jit(solution)/shard_map/ppermute | solution.py:133
  49.4 0.0 collective-permute-done.5
  49.4 0.1 add.35
  49.5 0.0 copy-start
  49.5 0.0 copy-start.1
  49.6 2.2 %collective-permute-done.2 = bf16[32,6656]{1,0:T(8,128)(2,1)S(1)} collective-permute-done((bf16[32,6656]{1,0:T(8,128)(2,1)S(1)}, bf16[32,6656]{1,0:T(8,128)(2,1)S(1)}, u32[]{:S(2)}, u32[]{:S(2)}) %collective-permute-start.2) | collective-permute-done | bytes 426016 | tf_op jit(solution)/shard_map/ppermute | solution.py:133
  51.8 0.0 collective-permute-done.3
  51.8 0.1 add.34
  51.9 2.4 %all_gather.21.refs_6_.f1 = bf16[64,6656]{1,0:T(8,128)(2,1)S(1)} all-gather(bf16[32,6656]{1,0:T(8,128)(2,1)S(1)} %add.35), channel_id=1, replica_groups={{0,1},{2,3},{4,5},{6,7},{8,9},{10,11},{12,13},{14,15},{16,17},{18,19},{..., dimensions={0}, use_global_device_ids=true | all-gather | bytes 1277952 | tf_op jit(solution)/shard_map/all_gather | solution.py:136
  54.3 2.4 %all_gather.20.refs_5_.f0 = bf16[64,6656]{1,0:T(8,128)(2,1)S(1)} all-gather(bf16[32,6656]{1,0:T(8,128)(2,1)S(1)} %add.34), channel_id=1, replica_groups={{0,1},{2,3},{4,5},{6,7},{8,9},{10,11},{12,13},{14,15},{16,17},{18,19},{..., dimensions={0}, use_global_device_ids=true | all-gather | bytes 1277952 | tf_op jit(solution)/shard_map/all_gather | solution.py:136
  56.7 0.0 collective-permute-done.6.refs_2_
  56.7 0.0 collective-permute-done.7.refs_9_
  56.7 1.8 %shard_map.50 = (bf16[64,3328]{1,0:T(8,128)(2,1)S(1)}, bf16[64,3328]{1,0:T(8,128)(2,1)S(1)}, bf16[128,3328]{1,0:T(8,128)(2,1)S(1)}) custom-call(s32[1]{0:T(128)} %bitcast.refs_0_.core, bf16[320,128]{1,0:T(8,128)(2,1)S(1)} %bitcast.4, bf16[320,128]{1,0:T(8,128)(2,1)S(1)} %collective-permute-done.6.refs_2_, bf16[64,6656]{1,0:T(8,128)(2,1)S(1)} %all_gather.18.refs_3_.n0, ...), custom_call_target="tpu_custom_call" | custom-call | flops 954204160 | bytes 6291456 | tf_op jit(solution)/shard_map/pallas_call | solution.py:74
  58.5 5.4 %collective-permute-start.10 = (bf16[64,3328]{1,0:T(8,128)(2,1)S(1)}, bf16[64,3328]{1,0:T(8,128)(2,1)S(1)}, u32[]{:S(2)}, u32[]{:S(2)}) collective-permute-start(bf16[64,3328]{1,0:T(8,128)(2,1)S(1)} %get-tuple-element.18), channel_id=1, source_target_pairs={{0,4},{1,1023},{2,6},{3,1021},{4,8},{5,1},{6,10},{7,3},{8,12},{9,5... | collective-permute-start | bytes 1277960 | tf_op jit(solution)/shard_map/ppermute | solution.py:133
  63.9 1.9 %shard_map.51 = (bf16[64,3328]{1,0:T(8,128)(2,1)S(1)}, bf16[64,3328]{1,0:T(8,128)(2,1)S(1)}, bf16[64,3328]{1,0:T(8,128)(2,1)S(1)}, bf16[128,3328]{1,0:T(8,128)(2,1)S(1)}) custom-call(s32[1]{0:T(128)} %bitcast.refs_0_.core, bf16[320,128]{1,0:T(8,128)(2,1)S(1)} %bitcast.5, bf16[320,128]{1,0:T(8,128)(2,1)S(1)} %collective-permute-done.6.refs_2_, ...), custom_call_target="tpu_custom_call" | custom-call | flops 954204160 | bytes 6291456 | tf_op jit(solution)/shard_map/pallas_call | solution.py:74
  65.8 3.6 %collective-permute-start.8 = (bf16[64,3328]{1,0:T(8,128)(2,1)S(1)}, bf16[64,3328]{1,0:T(8,128)(2,1)S(1)}, u32[]{:S(2)}, u32[]{:S(2)}) collective-permute-start(bf16[64,3328]{1,0:T(8,128)(2,1)S(1)} %get-tuple-element.16), channel_id=1, source_target_pairs={{0,4},{1,1023},{2,6},{3,1021},{4,8},{5,1},{6,10},{7,3},{8,12},{9,5... | collective-permute-start | bytes 1277960 | tf_op jit(solution)/shard_map/ppermute | solution.py:133
  69.4 0.0 collective-permute-done.10
  69.4 0.1 add_convert_fusion.2
  69.5 8.8 %collective-permute-start.11 = (bf16[64,3328]{1,0:T(8,128)(2,1)S(1)}, bf16[64,3328]{1,0:T(8,128)(2,1)S(1)}, u32[]{:S(2)}, u32[]{:S(2)}) collective-permute-start(bf16[64,3328]{1,0:T(8,128)(2,1)S(1)} %add_convert_fusion.2), channel_id=1, source_target_pairs={{0,4},{1,1023},{2,6},{3,1021},{4,8},{5,1},{6,10},{7,3},{8,12},{9,5... | collective-permute-start | bytes 1277960 | tf_op jit(solution)/shard_map/ppermute | solution.py:133
  78.3 0.0 collective-permute-done.8
  78.3 0.1 add_convert_fusion.3
  78.4 5.4 %collective-permute-start.9 = (bf16[64,3328]{1,0:T(8,128)(2,1)S(1)}, bf16[64,3328]{1,0:T(8,128)(2,1)S(1)}, u32[]{:S(2)}, u32[]{:S(2)}) collective-permute-start(bf16[64,3328]{1,0:T(8,128)(2,1)S(1)} %add_convert_fusion.3), channel_id=1, source_target_pairs={{0,4},{1,1023},{2,6},{3,1021},{4,8},{5,1},{6,10},{7,3},{8,12},{9,5... | collective-permute-start | bytes 1277960 | tf_op jit(solution)/shard_map/ppermute | solution.py:133
  83.8 0.0 collective-permute-done.11
  83.8 7.7 %collective-permute-start.12 = (bf16[64,3328]{1,0:T(8,128)(2,1)S(1)}, bf16[64,3328]{1,0:T(8,128)(2,1)S(1)}, u32[]{:S(2)}, u32[]{:S(2)}) collective-permute-start(bf16[64,3328]{1,0:T(8,128)(2,1)S(1)} %collective-permute-done.11), channel_id=1, source_target_pairs={{0,1},{1,0},{2,3},{3,2},{4,5},{5,4},{6,7},{7,6},{8,9},{9,8},{10,11... | collective-permute-start | bytes 1277960 | tf_op jit(solution)/shard_map/ppermute | solution.py:133
  91.5 1.9 %shard_map.52 = bf16[320,128]{1,0:T(8,128)(2,1)} custom-call(s32[1]{0:T(128)} %bitcast.refs_0_.core, bf16[64,6656]{1,0:T(8,128)(2,1)S(1)} %all_gather.18.refs_3_.n0, bf16[64,6656]{1,0:T(8,128)(2,1)S(1)} %all_gather.19.refs_4_.n1, bf16[64,6656]{1,0:T(8,128)(2,1)S(1)} %all_gather.20.refs_5_.f0, bf16[64,6656]{1,0:T(8,128)(2,1)S(1)} %all_gather.21.refs_6_.f1, ...), custom_call_target="tpu_custom_call" | custom-call | flops 545259520 | bytes 6291456 | tf_op jit(solution)/shard_map/pallas_call | solution.py:93
  93.4 0.0 collective-permute-done.9
  93.4 0.0 collective-permute-done.12
  93.4 0.2 add_convert_fusion.1
  93.6 24.6 %all_gather.22 = bf16[128,3328]{1,0:T(8,128)(2,1)S(1)} all-gather(bf16[64,3328]{1,0:T(8,128)(2,1)S(1)} %add_convert_fusion.1), channel_id=1, replica_groups={{0,2},{1,3},{4,6},{5,7},{8,10},{9,11},{12,14},{13,15},{16,18},{17,19},{..., dimensions={0}, use_global_device_ids=true | all-gather | bytes 1277952 | tf_op jit(solution)/shard_map/all_gather | solution.py:160
  118.2 0.1 add_convert_fusion
  118.3 2.5 %all_gather.23 = bf16[64,6656]{1,0:T(8,128)(2,1)S(1)} all-gather(bf16[64,3328]{1,0:T(8,128)(2,1)S(1)} %add_convert_fusion), channel_id=1, replica_groups={{0,1},{2,3},{4,5},{6,7},{8,9},{10,11},{12,13},{14,15},{16,17},{18,19},{..., dimensions={1}, use_global_device_ids=true | all-gather | bytes 1277952 | tf_op jit(solution)/shard_map/all_gather | solution.py:136
  120.8 0.9 copy.6
  (2 shorter events, 0.0 us)
Async XLA Ops:
  0.6 28.1 %collective-permute-start = (bf16[64,6656]{1,0:T(8,128)(2,1)}, bf16[64,6656]{1,0:T(8,128)(2,1)S(1)}, u32[]{:S(2)}, u32[]{:S(2)}) collective-permute-start(bf16[64,6656]{1,0:T(8,128)(2,1)} %w_own.1), channel_id=1, source_target_pairs={{0,4},{2,6},{4,8},{5,1},{6,10},{7,3},{8,12},{9,5},{10,14},{11,7},{... | collective-permute-start | bytes 2555912 | tf_op jit(solution)/shard_map/ppermute | solution.py:133
  1.9 36.1 %collective-permute-start.1 = (bf16[64,6656]{1,0:T(8,128)(2,1)}, bf16[64,6656]{1,0:T(8,128)(2,1)S(1)}, u32[]{:S(2)}, u32[]{:S(2)}) collective-permute-start(bf16[64,6656]{1,0:T(8,128)(2,1)} %w_own.1), channel_id=1, source_target_pairs={{1,1023},{3,1021},{60,64},{62,66},{65,61},{67,63},{124,128},{126,1... | collective-permute-start | bytes 2555912 | tf_op jit(solution)/shard_map/ppermute | solution.py:133
  26.8 29.9 %collective-permute-start.7 = (bf16[128,6656]{1,0:T(8,128)(2,1)}, bf16[128,6656]{1,0:T(8,128)(2,1)S(1)}, u32[]{:S(2)}, u32[]{:S(2)}) collective-permute-start(bf16[128,6656]{1,0:T(8,128)(2,1)} %refs_8_.3), channel_id=1, source_target_pairs={{0,1},{1,0},{2,3},{3,2},{4,5},{5,4},{6,7},{7,6},{8,9},{9,8},{10,11... | collective-permute-start | bytes 5111816 | tf_op jit(solution)/shard_map/ppermute | solution.py:133
  28.8 20.6 %collective-permute-start.5 = (bf16[32,6656]{1,0:T(8,128)(2,1)S(1)}, bf16[32,6656]{1,0:T(8,128)(2,1)S(1)}, u32[]{:S(2)}, u32[]{:S(2)}) collective-permute-start(bf16[32,6656]{1,0:T(8,128)(2,1)S(1)} %get-tuple-element.12), channel_id=1, source_target_pairs={{1,1023},{3,1021},{60,64},{62,66},{65,61},{67,63},{124,128},{126,1... | collective-permute-start | bytes 1277960 | tf_op jit(solution)/shard_map/ppermute | solution.py:133
  36.7 15.1 %collective-permute-start.3 = (bf16[32,6656]{1,0:T(8,128)(2,1)S(1)}, bf16[32,6656]{1,0:T(8,128)(2,1)S(1)}, u32[]{:S(2)}, u32[]{:S(2)}) collective-permute-start(bf16[32,6656]{1,0:T(8,128)(2,1)S(1)} %get-tuple-element.11), channel_id=1, source_target_pairs={{1,1023},{3,1021},{60,64},{62,66},{65,61},{67,63},{124,128},{126,1... | collective-permute-start | bytes 1277960 | tf_op jit(solution)/shard_map/ppermute | solution.py:133
  38.2 9.3 %copy-start.2 = (bf16[128,320]{0,1:T(8,128)(2,1)S(1)}, bf16[128,320]{0,1:T(8,128)(2,1)}, u32[]{:S(2)}) copy-start(bf16[128,320]{0,1:T(8,128)(2,1)} %param.3) | copy-start | bytes 245764
  38.2 9.3 %collective-permute-start.4 = (bf16[32,6656]{1,0:T(8,128)(2,1)S(1)}, bf16[32,6656]{1,0:T(8,128)(2,1)S(1)}, u32[]{:S(2)}, u32[]{:S(2)}) collective-permute-start(bf16[32,6656]{1,0:T(8,128)(2,1)S(1)} %get-tuple-element.20), channel_id=1, source_target_pairs={{0,4},{2,6},{4,8},{5,1},{6,10},{7,3},{8,12},{9,5},{10,14},{11,7},{... | collective-permute-start | bytes 1277960 | tf_op jit(solution)/shard_map/ppermute | solution.py:133
  39.6 12.1 %collective-permute-start.2 = (bf16[32,6656]{1,0:T(8,128)(2,1)S(1)}, bf16[32,6656]{1,0:T(8,128)(2,1)S(1)}, u32[]{:S(2)}, u32[]{:S(2)}) collective-permute-start(bf16[32,6656]{1,0:T(8,128)(2,1)S(1)} %get-tuple-element.21), channel_id=1, source_target_pairs={{0,4},{2,6},{4,8},{5,1},{6,10},{7,3},{8,12},{9,5},{10,14},{11,7},{... | collective-permute-start | bytes 1277960 | tf_op jit(solution)/shard_map/ppermute | solution.py:133
  47.5 9.2 %collective-permute-start.6 = (bf16[320,128]{1,0:T(8,128)(2,1)S(1)}, bf16[320,128]{1,0:T(8,128)(2,1)S(1)}, u32[]{:S(2)}, u32[]{:S(2)}) collective-permute-start(bf16[320,128]{1,0:T(8,128)(2,1)S(1)} %bitcast.3), channel_id=1, source_target_pairs={{0,1},{1,0},{2,3},{3,2},{4,5},{5,4},{6,7},{7,6},{8,9},{9,8},{10,11... | collective-permute-start | bytes 245768 | tf_op jit(solution)/shard_map/ppermute | solution.py:133
  49.5 7.2 %copy-start = (bf16[64,6656]{1,0:T(8,128)(2,1)S(1)}, bf16[64,6656]{1,0:T(8,128)(2,1)}, u32[]{:S(2)}) copy-start(bf16[64,6656]{1,0:T(8,128)(2,1)} %w_own.1) | copy-start | bytes 2555908
  49.5 7.2 %copy-start.1 = (bf16[128,6656]{1,0:T(8,128)(2,1)S(1)}, bf16[128,6656]{1,0:T(8,128)(2,1)}, u32[]{:S(2)}) copy-start(bf16[128,6656]{1,0:T(8,128)(2,1)} %refs_8_.3) | copy-start | bytes 5111812
  58.5 10.9 %collective-permute-start.10 = (bf16[64,3328]{1,0:T(8,128)(2,1)S(1)}, bf16[64,3328]{1,0:T(8,128)(2,1)S(1)}, u32[]{:S(2)}, u32[]{:S(2)}) collective-permute-start(bf16[64,3328]{1,0:T(8,128)(2,1)S(1)} %get-tuple-element.18), channel_id=1, source_target_pairs={{0,4},{1,1023},{2,6},{3,1021},{4,8},{5,1},{6,10},{7,3},{8,12},{9,5... | collective-permute-start | bytes 1277960 | tf_op jit(solution)/shard_map/ppermute | solution.py:133
  65.8 12.6 %collective-permute-start.8 = (bf16[64,3328]{1,0:T(8,128)(2,1)S(1)}, bf16[64,3328]{1,0:T(8,128)(2,1)S(1)}, u32[]{:S(2)}, u32[]{:S(2)}) collective-permute-start(bf16[64,3328]{1,0:T(8,128)(2,1)S(1)} %get-tuple-element.16), channel_id=1, source_target_pairs={{0,4},{1,1023},{2,6},{3,1021},{4,8},{5,1},{6,10},{7,3},{8,12},{9,5... | collective-permute-start | bytes 1277960 | tf_op jit(solution)/shard_map/ppermute | solution.py:133
  69.5 14.3 %collective-permute-start.11 = (bf16[64,3328]{1,0:T(8,128)(2,1)S(1)}, bf16[64,3328]{1,0:T(8,128)(2,1)S(1)}, u32[]{:S(2)}, u32[]{:S(2)}) collective-permute-start(bf16[64,3328]{1,0:T(8,128)(2,1)S(1)} %add_convert_fusion.2), channel_id=1, source_target_pairs={{0,4},{1,1023},{2,6},{3,1021},{4,8},{5,1},{6,10},{7,3},{8,12},{9,5... | collective-permute-start | bytes 1277960 | tf_op jit(solution)/shard_map/ppermute | solution.py:133
  78.4 15.0 %collective-permute-start.9 = (bf16[64,3328]{1,0:T(8,128)(2,1)S(1)}, bf16[64,3328]{1,0:T(8,128)(2,1)S(1)}, u32[]{:S(2)}, u32[]{:S(2)}) collective-permute-start(bf16[64,3328]{1,0:T(8,128)(2,1)S(1)} %add_convert_fusion.3), channel_id=1, source_target_pairs={{0,4},{1,1023},{2,6},{3,1021},{4,8},{5,1},{6,10},{7,3},{8,12},{9,5... | collective-permute-start | bytes 1277960 | tf_op jit(solution)/shard_map/ppermute | solution.py:133
  83.8 9.6 %collective-permute-start.12 = (bf16[64,3328]{1,0:T(8,128)(2,1)S(1)}, bf16[64,3328]{1,0:T(8,128)(2,1)S(1)}, u32[]{:S(2)}, u32[]{:S(2)}) collective-permute-start(bf16[64,3328]{1,0:T(8,128)(2,1)S(1)} %collective-permute-done.11), channel_id=1, source_target_pairs={{0,1},{1,0},{2,3},{3,2},{4,5},{5,4},{6,7},{7,6},{8,9},{9,8},{10,11... | collective-permute-start | bytes 1277960 | tf_op jit(solution)/shard_map/ppermute | solution.py:133
